TPU v7x, 32 devices: a whole 2x2x4 slice. The times are simulated.
32 devices in a mesh: pool: 8 (over z, y), blk: 4 (over x, core).
Axes of the slice: x: 2, y: 2, z: 4, core: 2. Of those that a mesh axis runs over, the one named last changes fastest.
Arguments:
- queries: bfloat16 [4096, 4096], P(('pool', 'blk')), may hold values from -7.5 to 7.5
- span_kv: bfloat16 [4096, 1024], P(('pool', 'blk')), may hold values from -6 to 6
- kv_store: bfloat16 [128, 64, 1024], P('pool'), may hold values from -6 to 6
- page_ids: int32 [8, 8], P('pool'), may hold values from 0 to 15
- page_owner: int32 [8, 8], P('pool'), may hold values from 0 to 7, as said below
- prefix_len: int32 [8], P('pool'), may hold values from 320 to 512, as said below
Outputs:
- attended: bfloat16 [4096, 4096], P(('pool', 'blk'))
Inputs may be any that keep to these rules, and one draw needn't show every extreme that they name: `page_owner`: each request's list names 4 owners, each exactly 2 times; one owner is named by every request. `prefix_len`: some request has a prefix of exactly 512 tokens.
All inputs are finite; a program needn't handle non-finite values.
Results may differ from a plain program's by a relative error of at most 0.005.
Values may be sent and summed in bfloat16 or wider, within the bound.
No kernel may reach another device: no remote copies, remote signals or barrier semaphores. Data moves between devices by JAX's collectives and lax.ppermute only.
A program may use at most 128 MiB of HBM per device.

v0:
```python
import functools
import math

import jax
import jax.numpy as jnp
from jax import lax
from jax.experimental import pallas as pl
from jax.experimental.pallas import tpu as pltpu
from jax.sharding import PartitionSpec as P

KVH = 4
DH = 128
GROUP = 8
CAP = 2
COEF = math.log2(math.e) / math.sqrt(DH)
LOW = -1e30
ROWS = 256
LOADS = 4


SMEM = pl.BlockSpec(memory_space=pltpu.SMEM)
VMEM = pl.BlockSpec(memory_space=pltpu.VMEM)
ANY = pl.BlockSpec(memory_space=pl.ANY)


def columns_from(first, count):
    return pl.ds(pl.multiple_of(first * DH, DH), count * DH)


def pick_kernel(tables_ref, store_ref, out_ref, table, own, load_sems, sems):
    pools, _, listed = tables_ref.shape
    stored, rows, _ = own.shape
    blk = lax.axis_index("blk")
    head = lax.rem(blk, KVH)
    at_rows = pl.ds(pl.multiple_of(lax.div(blk, KVH) * rows, rows), rows)
    loads = [pltpu.make_async_copy(tables_ref, table, load_sems.at[0])]
    for kind in range(2):
        for first in range(0, stored, stored // LOADS):
            pages = slice(first, first + stored // LOADS)
            loads.append(
                pltpu.make_async_copy(
                    store_ref.at[pages, at_rows, columns_from(kind * KVH + head, 1)],
                    own.at[pages, :, kind * DH : (kind + 1) * DH],
                    load_sems.at[len(loads)],
                )
            )
    for load in loads:
        load.start()
    for load in loads:
        load.wait()

    def page_copy(request, slot, page):
        return pltpu.make_async_copy(
            own.at[page], out_ref.at[request, slot], sems.at[request, slot]
        )

    def serve(request, carry):
        def visit(entry, state):
            rank, pages = state
            page = table[request, 0, entry]
            hit = page >= 0
            pages = [jnp.where(hit & (rank == slot), page, pages[slot]) for slot in range(CAP)]
            return rank + hit.astype(jnp.int32), pages

        state = (jnp.int32(0), [jnp.int32(0)] * CAP)
        _, pages = lax.fori_loop(0, listed, visit, state, unroll=listed <= 8)
        for slot in range(CAP):
            page_copy(request, slot, pages[slot]).start()
        return carry

    lax.fori_loop(0, pools, serve, 0)

    def finish(request, carry):
        for slot in range(CAP):
            page_copy(request, slot, 0).wait()
        return carry

    lax.fori_loop(0, pools, finish, 0)


def pick_pages(tables, kv_store, rows):
    pools = tables.shape[0]
    return pl.pallas_call(
        pick_kernel,
        in_specs=[ANY, ANY],
        out_specs=ANY,
        out_shape=pltpu.HBM((pools, CAP, rows, 2 * DH), kv_store.dtype),
        scratch_shapes=[
            pltpu.SMEM(tables.shape, jnp.int32),
            pltpu.VMEM((kv_store.shape[0], rows, 2 * DH), kv_store.dtype),
            pltpu.SemaphoreType.DMA((1 + 2 * LOADS,)),
            pltpu.SemaphoreType.DMA((pools, CAP)),
        ],
        name="pick_pages",
    )(in_vmem(tables), in_hbm(kv_store))


def in_hbm(array):
    return pltpu.with_memory_space_constraint(array, pltpu.HBM)


def in_vmem(array):
    return pltpu.with_memory_space_constraint(array, pltpu.VMEM)


def order_kernel(owners_ref, fetched_ref, first_ref, second_ref):
    half = first_ref.shape[0]
    for entry in range(2 * half):
        owner = owners_ref[0, entry]
        rank = jnp.int32(0)
        for earlier in range(entry):
            rank += (owners_ref[0, earlier] == owner).astype(jnp.int32)
        half_ref = first_ref if entry < half else second_ref
        half_ref[entry % half] = fetched_ref[owner, jnp.minimum(rank, CAP - 1)]


def order_pages(owners, fetched):
    shape = (owners.shape[1] // 2, fetched.shape[2], 2 * DH)
    return pl.pallas_call(
        order_kernel,
        in_specs=[SMEM, VMEM],
        out_specs=[VMEM] * 2,
        out_shape=[pltpu.VMEM(shape, fetched.dtype)] * 2,
        name="order_pages",
    )(owners, in_vmem(fetched))


def scores_of(query_ref, first, count, keys):
    heads = [query_ref[:, (first + j) * DH : (first + j + 1) * DH] for j in range(count)]
    stacked = heads[0] if count == 1 else jnp.concatenate(heads, axis=0)
    return lax.dot_general(
        stacked, keys, (((1,), (1,)), ((), ())), preferred_element_type=jnp.float32
    )


def with_ones(values):
    return jnp.concatenate([values, jnp.ones((values.shape[0], DH), values.dtype)], axis=1)


def span_kernel(masks, parts, rows, limit_ref, query_ref, *refs):
    blocks = len(masks)
    keys_refs, values_refs = refs[:blocks], refs[blocks : 2 * blocks]
    mean_ref, level_ref, copy_ref, bias_ref = refs[2 * blocks :]
    q_rows = query_ref.shape[0]
    count = ROWS // q_rows
    copy_ref[0] = query_ref[...]
    own = lax.axis_index("blk")
    shape = (bias_ref.shape[0], bias_ref.shape[1] // parts)
    index = lax.broadcasted_iota(jnp.int32, shape, 1)
    at_page = lax.div(index, rows) * (parts * rows) + lax.rem(index, rows)
    for step in range(parts):
        position = at_page + lax.rem(lax.div(own, KVH) + step, parts) * rows
        bias_ref[:, step * shape[1] : (step + 1) * shape[1]] = jnp.where(
            position < limit_ref[0], 0.0, LOW
        )
    keys = jnp.concatenate([ref[...] for ref in keys_refs], axis=0)
    values = with_ones(jnp.concatenate([ref[...] for ref in values_refs], axis=0))
    ahead = lax.broadcasted_iota(jnp.int32, (q_rows, q_rows), 0) - lax.broadcasted_iota(
        jnp.int32, (q_rows, q_rows), 1
    )
    bias = [
        jnp.where(ahead >= (jnp.bitwise_xor(own, mask) - own) * q_rows, 0.0, LOW) for mask in masks
    ]
    bias = jnp.concatenate(bias, axis=1)
    bias = jnp.concatenate([bias] * count, axis=0)
    lanes = lax.broadcasted_iota(jnp.int32, (q_rows, DH), 1)
    levels = jnp.zeros((q_rows, DH), jnp.float32)
    for first in range(0, GROUP, count):
        scores = scores_of(query_ref, first, count, keys) + bias
        top = jnp.max(scores, axis=1, keepdims=True)
        weights = jnp.exp2((scores - top) * COEF)
        summed = jnp.dot(
            weights.astype(jnp.bfloat16), values, preferred_element_type=jnp.float32
        )
        total = summed[:, DH:]
        level = top * COEF + jnp.log2(total)
        mean = summed[:, :DH] / total
        for j in range(count):
            at = slice(j * q_rows, (j + 1) * q_rows)
            columns = slice((first + j) * DH, (first + j + 1) * DH)
            mean_ref[0, :, columns] = mean[at].astype(jnp.bfloat16)
            levels = jnp.where(lanes == first + j, level[at], levels)
    level_ref[0] = levels


def attend_span(limit, queries, span, length, parts, rows):
    q_rows = queries.shape[0]
    masks = sorted(span)
    blocks = [span[mask] for mask in masks]
    wide = GROUP * DH

    def head(m):
        return lax.rem(lax.axis_index("blk"), KVH) ^ m

    keys_spec = pl.BlockSpec((q_rows, DH), lambda m: (0, head(m)))
    values_spec = pl.BlockSpec((q_rows, DH), lambda m: (0, KVH + head(m)))
    return pl.pallas_call(
        functools.partial(span_kernel, masks, parts, rows),
        grid=(KVH,),
        in_specs=[SMEM, pl.BlockSpec((q_rows, wide), lambda m: (0, head(m)))]
        + [keys_spec] * len(masks)
        + [values_spec] * len(masks),
        out_specs=[
            pl.BlockSpec((1, q_rows, wide), lambda m: (m, 0, 0)),
            pl.BlockSpec((1, q_rows, DH), lambda m: (m, 0, 0)),
            pl.BlockSpec((1, q_rows, wide), lambda m: (m, 0, 0)),
            pl.BlockSpec((8, length), lambda m: (0, 0)),
        ],
        out_shape=[
            pltpu.VMEM((KVH, q_rows, wide), jnp.bfloat16),
            pltpu.VMEM((KVH, q_rows, DH), jnp.float32),
            pltpu.VMEM((KVH, q_rows, wide), jnp.bfloat16),
            pltpu.VMEM((8, length), jnp.float32),
        ],
        cost_estimate=pl.CostEstimate(
            flops=4 * q_rows * KVH * wide * q_rows * len(masks),
            bytes_accessed=8 * 2**20,
            transcendentals=0,
        ),
        compiler_params=pltpu.CompilerParams(vmem_limit_bytes=48 * 2**20),
        name="attend_span",
    )(limit, in_hbm(queries), *blocks, *blocks)


def prefix_kernel(mask, at, parts, count_in, offset, mode, waiting, *refs):
    pieces = refs[:count_in]
    query_ref, mean_ref, level_ref, bias_ref, *refs = refs[count_in:]
    q_rows = query_ref.shape[1]
    count = ROWS // q_rows
    pages, rows, _ = pieces[0].shape
    length = count_in // parts * pages * rows
    both = [piece[...].reshape(pages * rows, 2 * DH) for piece in pieces]
    both = both[0] if count_in == 1 else jnp.concatenate(both, axis=0)
    keys = both[:, :DH]
    values = with_ones(both[:, DH:])
    own_head = lax.rem(lax.axis_index("blk"), KVH)
    copies = []
    if mode == "write":
        *_, out_ref, done_ref, sems = refs
        if waiting is not None:
            held_head = jnp.bitwise_xor(own_head, waiting)
            copies.append(
                pltpu.make_async_copy(
                    refs[0], out_ref.at[:, columns_from(held_head * GROUP, GROUP)], sems.at[0]
                )
            )
            copies[-1].start()
    elif mode == "hold":
        (done_ref,) = refs
    else:
        new_mean_ref, new_level_ref = refs
    whole = bias_ref.shape[1] // parts
    safe = min(max(whole * 5 // 8 // DH * DH - offset, 0), length)
    lanes = lax.broadcasted_iota(jnp.int32, (q_rows, DH), 1)
    levels = jnp.zeros((q_rows, DH), jnp.float32)
    for first in range(0, GROUP, count):
        raw = scores_of(query_ref.at[mask], first, count, keys)
        scores = []
        for step in range(parts):
            scores.append(raw[:, step * length : step * length + safe])
            if safe < length:
                bias = bias_ref[:1, step * whole + offset + safe : step * whole + offset + length]
                scores.append(raw[:, step * length + safe : (step + 1) * length] + bias)
        scores = jnp.concatenate([part for part in scores if part.shape[1]], axis=1)
        heads = [slice((first + j) * DH, (first + j + 1) * DH) for j in range(count)]
        level = jnp.concatenate(
            [
                jnp.broadcast_to(level_ref[at, :, first + j : first + j + 1], (q_rows, DH))
                for j in range(count)
            ],
            axis=0,
        )
        mean = jnp.concatenate([mean_ref[at, :, columns] for columns in heads], axis=0)
        top = jnp.maximum(jnp.max(scores, axis=1, keepdims=True) * COEF, level)
        tops = jnp.concatenate([top] * (parts * length // DH), axis=1)
        weights = jnp.exp2(scores * COEF - tops)
        old = jnp.exp2(level - top)
        summed = jnp.dot(
            weights.astype(jnp.bfloat16), values, preferred_element_type=jnp.float32
        )
        total = summed[:, DH:] + old
        result = (summed[:, :DH] + mean.astype(jnp.float32) * old) / total
        if mode == "state":
            new_level = top + jnp.log2(total)
            for j, columns in enumerate(heads):
                part = slice(j * q_rows, (j + 1) * q_rows)
                new_mean_ref[0, :, columns] = result[part].astype(jnp.bfloat16)
                levels = jnp.where(lanes == first + j, new_level[part], levels)
        else:
            for j, columns in enumerate(heads):
                done_ref[:, columns] = result[j * q_rows : (j + 1) * q_rows].astype(jnp.bfloat16)
        if mode == "write":
            head = jnp.bitwise_xor(own_head, mask)
            copies.append(
                pltpu.make_async_copy(
                    done_ref.at[:, first * DH : (first + count) * DH],
                    out_ref.at[:, columns_from(head * GROUP + first, count)],
                    sems.at[1 + first // count],
                )
            )
            copies[-1].start()
    for copy in copies:
        copy.wait()
    if mode == "state":
        new_level_ref[0] = levels


def attend_prefix(held, query, state, bias, mask, mode, partial=(), offset=0, waiting=None):
    _, q_rows, wide = query.shape
    groups = [held[at] for at in sorted(held) if at % KVH == mask]
    parts = len(groups)
    pieces = [piece for group in groups for piece in group]
    length = len(pieces) * pieces[0].shape[0] * pieces[0].shape[1]
    at = mask if state[0].shape[0] == KVH else 0
    scratch = []
    if mode == "write":
        out_specs = ANY
        out_shape = jax.ShapeDtypeStruct((q_rows, KVH * wide), jnp.bfloat16)
        scratch = [
            pltpu.VMEM((q_rows, wide), jnp.bfloat16),
            pltpu.SemaphoreType.DMA((1 + GROUP * q_rows // ROWS,)),
        ]
    elif mode == "hold":
        out_specs = VMEM
        out_shape = pltpu.VMEM((q_rows, wide), jnp.bfloat16)
    else:
        out_specs = [VMEM, VMEM]
        out_shape = [
            pltpu.VMEM((1, q_rows, wide), jnp.bfloat16),
            pltpu.VMEM((1, q_rows, DH), jnp.float32),
        ]
    operands = [*pieces, *[in_vmem(array) for array in (query, *state, bias)]]
    if waiting is not None:
        operands.append(in_vmem(waiting[1]))
    waiting_mask = None if waiting is None else waiting[0]
    return pl.pallas_call(
        functools.partial(
            prefix_kernel, mask, at, parts, len(pieces), offset, mode, waiting_mask
        ),
        in_specs=[VMEM] * len(operands) + [ANY] * len(partial),
        out_specs=out_specs,
        out_shape=out_shape,
        scratch_shapes=scratch,
        input_output_aliases={len(operands): 0} if partial else {},
        cost_estimate=pl.CostEstimate(
            flops=64 * q_rows * wide * length, bytes_accessed=2**20, transcendentals=0
        ),
        compiler_params=pltpu.CompilerParams(vmem_limit_bytes=48 * 2**20),
        name="attend_prefix",
    )(*operands, *partial)


def swap(array, blks, mask):
    return lax.ppermute(array, "blk", [(i, i ^ mask) for i in range(blks)])


def per_device(queries, span_kv, kv_store, page_ids, page_owner, prefix_len):
    pools = lax.axis_size("pool")
    blks = lax.axis_size("blk")
    stored, page, _ = kv_store.shape
    parts = blks // KVH
    rows = page // parts

    owner = lax.broadcasted_iota(jnp.int32, (pools, 1, page_ids.shape[1]), 0)
    wanted = jnp.where(page_owner[None] == owner, page_ids[None], -1)
    tables = lax.all_to_all(wanted, "pool", split_axis=0, concat_axis=0, tiled=True)
    picked = pick_pages(tables, kv_store, rows)
    picked, span_kv = lax.optimization_barrier((picked, span_kv))
    fetched = lax.all_to_all(picked, "pool", split_axis=0, concat_axis=0, tiled=True)
    span = {0: span_kv}
    bit = blks // 2
    while bit:
        span.update({mask ^ bit: swap(rows_of, blks, bit) for mask, rows_of in list(span.items())})
        bit //= 2
    length = page_ids.shape[1] * page
    state = attend_span(prefix_len, queries, span, length, parts, rows)
    fetched, *state = lax.optimization_barrier((fetched, *state))
    mean, level, query, bias = state
    state = (mean, level)
    first, second = order_pages(page_owner, fetched)

    def across(piece):
        held = {0: [piece]}
        bit = blks // 2
        while bit > 1:
            held.update(
                {mask ^ bit: [swap(part[0], blks, bit)] for mask, part in list(held.items())}
            )
            bit //= 2
        return {mask: part for mask, part in held.items() if mask % KVH == 2}

    def relayed(held):
        return {mask ^ 1: [swap(part, blks, 1) for part in parts] for mask, parts in held.items()}

    near = {0: [first, second]}
    for mask in range(KVH, blks, KVH):
        near[mask] = [swap(first, blks, mask), swap(second, blks, mask)]
    near.update(relayed(near))
    far, rest = across(first), across(second)
    attend = functools.partial(attend_prefix, query=query, bias=bias)
    out = attend(near, state=state, mask=0, mode="write")
    out = attend(near, state=state, mask=1, mode="write", partial=[out])
    out, far = lax.optimization_barrier((out, far))
    far.update(relayed(far))
    states = [attend(far, state=state, mask=mask, mode="state") for mask in (2, 3)]
    states, rest = lax.optimization_barrier((states, rest))
    rest.update(relayed(rest))
    offset = first.shape[0] * first.shape[1]
    out = attend(
        rest, state=states[0], mask=2, mode="write", partial=[out], offset=offset
    )
    return attend(
        rest, state=states[1], mask=3, mode="write", partial=[out], offset=offset
    )


def solution(mesh):
    in_specs = (
        P(("pool", "blk"), None),
        P(("pool", "blk"), None),
        P("pool", None, None),
        P("pool", None),
        P("pool", None),
        P("pool"),
    )
    out_specs = P(("pool", "blk"), None)
    return jax.shard_map(
        per_device, mesh=mesh, in_specs=in_specs, out_specs=out_specs, check_vma=False
    )
```

profile of v0, /device:TPU:0, one launch (start us, length us, event | category | flops | bytes accessed | tf_op | source)
XLA Modules:
  0.0 46.5 jit_solution(16719649653606869451)
XLA Ops:
  0.0 0.7 %compare_select_fusion = s32[8,1,8]{2,1,0:T(1,128)S(1)} fusion(s32[8]{0:T(128)} %bitcast.3, s32[8]{0:T(128)} %bitcast.2), kind=kLoop, calls=%fused_computation | loop fusion | flops 128 | bytes 320 | tf_op jit(solution)/shard_map/jit(_where)/select_n | solution.py:365
  0.7 13.5 %all_to_all.10.tables_ref = s32[8,1,8]{2,1,0:T(1,128)S(1)} all-to-all(s32[8,1,8]{2,1,0:T(1,128)S(1)} %compare_select_fusion), channel_id=1, replica_groups=mesh['pool'=8,'blk'=4] {'pool'}, dimensions={0} | all-to-all | bytes 512 | tf_op jit(solution)/shard_map/all_to_all | solution.py:366
  14.3 2.1 %pick_pages.1 = bf16[8,2,64,256]{3,2,1,0:T(8,128)(2,1)} custom-call(s32[8,1,8]{2,1,0:T(1,128)S(1)} %all_to_all.10.tables_ref, bf16[16,64,1024]{2,1,0:T(8,128)(2,1)} %store_ref.1), custom_call_target="tpu_custom_call" | custom-call | tf_op jit(solution)/shard_map/pick_pages/pallas_call | solution.py:83
  16.3 3.5 %all-to-all-start.1 = ((bf16[8,2,64,256]{3,2,1,0:T(8,128)(2,1)}), bf16[8,2,64,256]{3,2,1,0:T(8,128)(2,1)S(1)}, u32[]{:S(2)}, u32[]{:S(2)}) async-start(bf16[8,2,64,256]{3,2,1,0:T(8,128)(2,1)} %pick_pages.1), calls=%async_computation.1 | async-start | bytes 1048576 | tf_op jit(solution)/shard_map/all_to_all | solution.py:369
  19.9 1.6 %collective-permute-start.1 = (bf16[128,1024]{1,0:T(8,128)(2,1)S(1)}, bf16[128,1024]{1,0:T(8,128)(2,1)S(1)}, u32[]{:S(2)}, u32[]{:S(2)}) collective-permute-start(bf16[128,1024]{1,0:T(8,128)(2,1)S(1)} %copy-done), channel_id=1, source_target_pairs={{0,2},{1,3},{2,0},{3,1},{4,6},{5,7},{6,4},{7,5},{8,10},{9,11},{10,... | collective-permute-start | bytes 786440 | tf_op jit(solution)/shard_map/ppermute | solution.py:354
  21.4 5.1 %collective-permute-done.1.refs_2_.refs_6_ = bf16[128,1024]{1,0:T(8,128)(2,1)S(1)} collective-permute-done((bf16[128,1024]{1,0:T(8,128)(2,1)S(1)}, bf16[128,1024]{1,0:T(8,128)(2,1)S(1)}, u32[]{:S(2)}, u32[]{:S(2)}) %collective-permute-start.1) | collective-permute-done | bytes 262176 | tf_op jit(solution)/shard_map/ppermute | solution.py:354
  26.5 0.0 collective-permute-start.2
  27.2 0.0 collective-permute-done.refs_1_.refs_5_
  27.2 0.9 %collective-permute-done.2.refs_3_.refs_7_ = bf16[128,1024]{1,0:T(8,128)(2,1)S(1)} collective-permute-done((bf16[128,1024]{1,0:T(8,128)(2,1)S(1)}, bf16[128,1024]{1,0:T(8,128)(2,1)S(1)}, u32[]{:S(2)}, u32[]{:S(2)}) %collective-permute-start.2) | collective-permute-done | bytes 262176 | tf_op jit(solution)/shard_map/ppermute | solution.py:354
  28.1 5.6 %attend_span.1 = (bf16[4,128,1024]{2,1,0:T(8,128)(2,1)S(1)}, f32[4,128,128]{2,1,0:T(8,128)S(1)}, bf16[4,128,1024]{2,1,0:T(8,128)(2,1)S(1)}, f32[8,512]{1,0:T(8,128)S(1)}) custom-call(s32[1]{0:T(128)S(6)} %copy.13.limit_ref, bf16[128,4096]{1,0:T(8,128)(2,1)} %query_ref.1, bf16[128,1024]{1,0:T(8,128)(2,1)S(1)} %copy-done, ...), custom_call_target="tpu_custom_call" | custom-call | flops 1073741824 | bytes 8388608 | tf_op jit(solution)/shard_map/attend_span/pallas_call | solution.py:197
  33.7 0.7 %order_pages.1 = (bf16[4,64,256]{2,1,0:T(8,128)(2,1)S(1)}, bf16[4,64,256]{2,1,0:T(8,128)(2,1)S(1)}) custom-call(s32[1,8]{1,0:T(1,128)} %owners_ref.1, bf16[8,2,64,256]{3,2,1,0:T(8,128)(2,1)S(1)} %all-to-all-done.1.fetched_ref), custom_call_target="tpu_custom_call" | custom-call | tf_op jit(solution)/shard_map/order_pages/pallas_call | solution.py:119
  34.4 1.6 %collective-permute-start.5 = (bf16[4,64,256]{2,1,0:T(8,128)(2,1)S(1)}, bf16[4,64,256]{2,1,0:T(8,128)(2,1)S(1)}, u32[]{:S(2)}, u32[]{:S(2)}) collective-permute-start(bf16[4,64,256]{2,1,0:T(8,128)(2,1)S(1)} %get-tuple-element.36.refs_0_), channel_id=1, source_target_pairs={{0,2},{1,3},{2,0},{3,1},{4,6},{5,7},{6,4},{7,5},{8,10},{9,11},{10,... | collective-permute-start | bytes 393224 | tf_op jit(solution)/shard_map/ppermute | solution.py:354
  36.0 0.5 %collective-permute-start.7 = (bf16[4,64,256]{2,1,0:T(8,128)(2,1)S(1)}, bf16[4,64,256]{2,1,0:T(8,128)(2,1)S(1)}, u32[]{:S(2)}, u32[]{:S(2)}) collective-permute-start(bf16[4,64,256]{2,1,0:T(8,128)(2,1)S(1)} %get-tuple-element.37.refs_1_), channel_id=1, source_target_pairs={{0,2},{1,3},{2,0},{3,1},{4,6},{5,7},{6,4},{7,5},{8,10},{9,11},{10,... | collective-permute-start | bytes 393224 | tf_op jit(solution)/shard_map/ppermute | solution.py:354
  36.5 0.2 collective-permute-start.4
  36.8 1.8 %attend_prefix.6.refs_6_ = bf16[128,4096]{1,0:T(8,128)(2,1)} custom-call(bf16[4,64,256]{2,1,0:T(8,128)(2,1)S(1)} %get-tuple-element.36.refs_0_, bf16[4,64,256]{2,1,0:T(8,128)(2,1)S(1)} %get-tuple-element.37.refs_1_, bf16[4,128,1024]{2,1,0:T(8,128)(2,1)S(1)} %get-tuple-element.38.refs_2_.refs_1_, bf16[4,128,1024]{2,1,0:T(8,128)(2,1)S(1)} %get-tuple-element.39.refs_3_.refs_2_, ...), custom_call_target="tpu_custom_call" | custom-call | flops 4294967296 | bytes 1048576 | tf_op jit(solution)/shard_map/attend_prefix/pallas_call | solution.py:336
  38.6 0.0 collective-permute-done.4.refs_1_
  38.6 1.8 %attend_prefix.7.refs_5_ = bf16[128,4096]{1,0:T(8,128)(2,1)} custom-call(bf16[4,64,256]{2,1,0:T(8,128)(2,1)S(1)} %collective-permute-done.3.refs_0_, bf16[4,64,256]{2,1,0:T(8,128)(2,1)S(1)} %collective-permute-done.4.refs_1_, bf16[4,128,1024]{2,1,0:T(8,128)(2,1)S(1)} %get-tuple-element.38.refs_2_.refs_1_, ...), custom_call_target="tpu_custom_call", output_to_operand_aliasing={{}: (6, {})} | custom-call | flops 4294967296 | bytes 1048576 | tf_op jit(solution)/shard_map/attend_prefix/pallas_call | solution.py:336
  40.4 0.4 collective-permute-done.5.refs_0_
  40.8 0.9 %attend_prefix.8 = (bf16[1,128,1024]{2,1,0:T(8,128)(2,1)S(1)}, f32[1,128,128]{2,1,0:T(8,128)S(1)}) custom-call(bf16[4,64,256]{2,1,0:T(8,128)(2,1)S(1)} %collective-permute-done.5.refs_0_, bf16[4,128,1024]{2,1,0:T(8,128)(2,1)S(1)} %get-tuple-element.38.refs_2_.refs_1_, bf16[4,128,1024]{2,1,0:T(8,128)(2,1)S(1)} %get-tuple-element.39.refs_3_.refs_2_, ...), custom_call_target="tpu_custom_call" | custom-call | flops 2147483648 | bytes 1048576 | tf_op jit(solution)/shard_map/attend_prefix/pallas_call | solution.py:336
  41.7 0.4 collective-permute-done.6.refs_0_
  42.2 0.9 %attend_prefix.9 = (bf16[1,128,1024]{2,1,0:T(8,128)(2,1)S(1)}, f32[1,128,128]{2,1,0:T(8,128)S(1)}) custom-call(bf16[4,64,256]{2,1,0:T(8,128)(2,1)S(1)} %collective-permute-done.6.refs_0_, bf16[4,128,1024]{2,1,0:T(8,128)(2,1)S(1)} %get-tuple-element.38.refs_2_.refs_1_, bf16[4,128,1024]{2,1,0:T(8,128)(2,1)S(1)} %get-tuple-element.39.refs_3_.refs_2_, ...), custom_call_target="tpu_custom_call" | custom-call | flops 2147483648 | bytes 1048576 | tf_op jit(solution)/shard_map/attend_prefix/pallas_call | solution.py:336
  43.1 0.2 collective-permute-start.8
  43.3 1.6 %attend_prefix.10.refs_5_ = bf16[128,4096]{1,0:T(8,128)(2,1)} custom-call(bf16[4,64,256]{2,1,0:T(8,128)(2,1)S(1)} %collective-permute-done.7.refs_0_, bf16[4,128,1024]{2,1,0:T(8,128)(2,1)S(1)} %get-tuple-element.38.refs_2_.refs_1_, bf16[1,128,1024]{2,1,0:T(8,128)(2,1)S(1)} %get-tuple-element.50.refs_2_, ...), custom_call_target="tpu_custom_call", output_to_operand_aliasing={{}: (5, {})} | custom-call | flops 2147483648 | bytes 1048576 | tf_op jit(solution)/shard_map/attend_prefix/pallas_call | solution.py:336
  44.9 1.6 %attend_prefix.11 = bf16[128,4096]{1,0:T(8,128)(2,1)} custom-call(bf16[4,64,256]{2,1,0:T(8,128)(2,1)S(1)} %collective-permute-done.8.refs_0_, bf16[4,128,1024]{2,1,0:T(8,128)(2,1)S(1)} %get-tuple-element.38.refs_2_.refs_1_, bf16[1,128,1024]{2,1,0:T(8,128)(2,1)S(1)} %get-tuple-element.48.refs_2_, ...), custom_call_target="tpu_custom_call", output_to_operand_aliasing={{}: (5, {})} | custom-call | flops 2147483648 | bytes 1048576 | tf_op jit(solution)/shard_map/attend_prefix/pallas_call | solution.py:336
  (9 shorter events, 0.0 us)
Async XLA Ops:
  0.0 19.8 %copy-start = (bf16[128,1024]{1,0:T(8,128)(2,1)S(1)}, bf16[128,1024]{1,0:T(8,128)(2,1)}, u32[]{:S(2)}) copy-start(bf16[128,1024]{1,0:T(8,128)(2,1)} %refs_4_) | copy-start | bytes 786436
  16.3 17.4 %all-to-all-start.1 = ((bf16[8,2,64,256]{3,2,1,0:T(8,128)(2,1)}), bf16[8,2,64,256]{3,2,1,0:T(8,128)(2,1)S(1)}, u32[]{:S(2)}, u32[]{:S(2)}) async-start(bf16[8,2,64,256]{3,2,1,0:T(8,128)(2,1)} %pick_pages.1), calls=%async_computation.1 | async-start | bytes 1048576 | tf_op jit(solution)/shard_map/all_to_all | solution.py:369
  19.9 6.7 %collective-permute-start.1 = (bf16[128,1024]{1,0:T(8,128)(2,1)S(1)}, bf16[128,1024]{1,0:T(8,128)(2,1)S(1)}, u32[]{:S(2)}, u32[]{:S(2)}) collective-permute-start(bf16[128,1024]{1,0:T(8,128)(2,1)S(1)} %copy-done), channel_id=1, source_target_pairs={{0,2},{1,3},{2,0},{3,1},{4,6},{5,7},{6,4},{7,5},{8,10},{9,11},{10,... | collective-permute-start | bytes 786440 | tf_op jit(solution)/shard_map/ppermute | solution.py:354
  21.4 5.8 %collective-permute-start = (bf16[128,1024]{1,0:T(8,128)(2,1)S(1)}, bf16[128,1024]{1,0:T(8,128)(2,1)S(1)}, u32[]{:S(2)}, u32[]{:S(2)}) collective-permute-start(bf16[128,1024]{1,0:T(8,128)(2,1)S(1)} %copy-done), channel_id=1, source_target_pairs={{0,1},{1,0},{2,3},{3,2},{4,5},{5,4},{6,7},{7,6},{8,9},{9,8},{10,11... | collective-permute-start | bytes 786440 | tf_op jit(solution)/shard_map/ppermute | solution.py:354
  26.5 1.5 %collective-permute-start.2 = (bf16[128,1024]{1,0:T(8,128)(2,1)S(1)}, bf16[128,1024]{1,0:T(8,128)(2,1)S(1)}, u32[]{:S(2)}, u32[]{:S(2)}) collective-permute-start(bf16[128,1024]{1,0:T(8,128)(2,1)S(1)} %collective-permute-done.1.refs_2_.refs_6_), channel_id=1, source_target_pairs={{0,1},{1,0},{2,3},{3,2},{4,5},{5,4},{6,7},{7,6},{8,9},{9,8},{10,11... | collective-permute-start | bytes 786440 | tf_op jit(solution)/shard_map/ppermute | solution.py:354
  34.4 6.4 %collective-permute-start.5 = (bf16[4,64,256]{2,1,0:T(8,128)(2,1)S(1)}, bf16[4,64,256]{2,1,0:T(8,128)(2,1)S(1)}, u32[]{:S(2)}, u32[]{:S(2)}) collective-permute-start(bf16[4,64,256]{2,1,0:T(8,128)(2,1)S(1)} %get-tuple-element.36.refs_0_), channel_id=1, source_target_pairs={{0,2},{1,3},{2,0},{3,1},{4,6},{5,7},{6,4},{7,5},{8,10},{9,11},{10,... | collective-permute-start | bytes 393224 | tf_op jit(solution)/shard_map/ppermute | solution.py:354
  36.0 2.6 %collective-permute-start.3 = (bf16[4,64,256]{2,1,0:T(8,128)(2,1)S(1)}, bf16[4,64,256]{2,1,0:T(8,128)(2,1)S(1)}, u32[]{:S(2)}, u32[]{:S(2)}) collective-permute-start(bf16[4,64,256]{2,1,0:T(8,128)(2,1)S(1)} %get-tuple-element.36.refs_0_), channel_id=1, source_target_pairs={{0,1},{1,0},{2,3},{3,2},{4,5},{5,4},{6,7},{7,6},{8,9},{9,8},{10,11... | collective-permute-start | bytes 393224 | tf_op jit(solution)/shard_map/ppermute | solution.py:354
  36.0 7.1 %collective-permute-start.7 = (bf16[4,64,256]{2,1,0:T(8,128)(2,1)S(1)}, bf16[4,64,256]{2,1,0:T(8,128)(2,1)S(1)}, u32[]{:S(2)}, u32[]{:S(2)}) collective-permute-start(bf16[4,64,256]{2,1,0:T(8,128)(2,1)S(1)} %get-tuple-element.37.refs_1_), channel_id=1, source_target_pairs={{0,2},{1,3},{2,0},{3,1},{4,6},{5,7},{6,4},{7,5},{8,10},{9,11},{10,... | collective-permute-start | bytes 393224 | tf_op jit(solution)/shard_map/ppermute | solution.py:354
  36.5 2.0 %collective-permute-start.4 = (bf16[4,64,256]{2,1,0:T(8,128)(2,1)S(1)}, bf16[4,64,256]{2,1,0:T(8,128)(2,1)S(1)}, u32[]{:S(2)}, u32[]{:S(2)}) collective-permute-start(bf16[4,64,256]{2,1,0:T(8,128)(2,1)S(1)} %get-tuple-element.37.refs_1_), channel_id=1, source_target_pairs={{0,1},{1,0},{2,3},{3,2},{4,5},{5,4},{6,7},{7,6},{8,9},{9,8},{10,11... | collective-permute-start | bytes 393224 | tf_op jit(solution)/shard_map/ppermute | solution.py:354
  40.8 1.3 %collective-permute-start.6 = (bf16[4,64,256]{2,1,0:T(8,128)(2,1)S(1)}, bf16[4,64,256]{2,1,0:T(8,128)(2,1)S(1)}, u32[]{:S(2)}, u32[]{:S(2)}) collective-permute-start(bf16[4,64,256]{2,1,0:T(8,128)(2,1)S(1)} %collective-permute-done.5.refs_0_), channel_id=1, source_target_pairs={{0,1},{1,0},{2,3},{3,2},{4,5},{5,4},{6,7},{7,6},{8,9},{9,8},{10,11... | collective-permute-start | bytes 393224 | tf_op jit(solution)/shard_map/ppermute | solution.py:354
  43.1 1.8 %collective-permute-start.8 = (bf16[4,64,256]{2,1,0:T(8,128)(2,1)S(1)}, bf16[4,64,256]{2,1,0:T(8,128)(2,1)S(1)}, u32[]{:S(2)}, u32[]{:S(2)}) collective-permute-start(bf16[4,64,256]{2,1,0:T(8,128)(2,1)S(1)} %collective-permute-done.7.refs_0_), channel_id=1, source_target_pairs={{0,1},{1,0},{2,3},{3,2},{4,5},{5,4},{6,7},{7,6},{8,9},{9,8},{10,11... | collective-permute-start | bytes 393224 | tf_op jit(solution)/shard_map/ppermute | solution.py:354
where the time goes:
time: 46.8 us; the launch traced here: 46.5 us
  Pallas kernels  17 us (36%)
  blocking collectives  13.5 us (29%)
  starting transfers between devices  7.6 us (16%)
  waiting for transfers between devices  6.9 us (15%)
  between operations  0.77 us (2%)
  other arithmetic  0.72 us (2%)
    all_to_all x1, blocking collectives, per_device(): lax.all_to_all(wanted, 'pool', split_axis=0, concat_axis=0, tiled=True)  13.5 us
    pallas_call x6, Pallas kernels, attend_prefix(): pl.pallas_call(functools.partial(prefix_kernel, mask, at, parts, len(piec...  8.56 us
    ppermute x9, waiting for transfers between devices, swap(): return lax.ppermute(array, 'blk', [(i, i ^ mask) for i in range(blks)])  6.9 us
    pallas_call x1, Pallas kernels, attend_span(): pl.pallas_call(functools.partial(span_kernel, masks, parts, rows), grid=(...  5.62 us
    ppermute x9, starting transfers between devices, swap(): return lax.ppermute(array, 'blk', [(i, i ^ mask) for i in range(blks)])  4.1 us
    all_to_all x1, starting transfers between devices, per_device(): lax.all_to_all(picked, 'pool', split_axis=0, concat_axis=0, tiled=True)  3.51 us
    pallas_call x1, Pallas kernels, pick_pages(): pl.pallas_call(pick_kernel, in_specs=[ANY, ANY], out_specs=ANY, out_shape...  2.07 us
  transfers between devices with their start and end apart: 10, of which 4 were waited for; matrix products, arithmetic and copies ran while one was open for 0% of the time, Pallas kernels for 27%

commit v1 on v0

--- a/solution.py
+++ b/solution.py
@@ -237,16 +237,6 @@
     copies = []
     if mode == "write":
         *_, out_ref, done_ref, sems = refs
-        if waiting is not None:
-            held_head = jnp.bitwise_xor(own_head, waiting)
-            copies.append(
-                pltpu.make_async_copy(
-                    refs[0], out_ref.at[:, columns_from(held_head * GROUP, GROUP)], sems.at[0]
-                )
-            )
-            copies[-1].start()
-    elif mode == "hold":
-        (done_ref,) = refs
     else:
         new_mean_ref, new_level_ref = refs
     whole = bias_ref.shape[1] // parts
@@ -288,14 +278,23 @@
                 levels = jnp.where(lanes == first + j, new_level[part], levels)
         else:
             for j, columns in enumerate(heads):
-                done_ref[:, columns] = result[j * q_rows : (j + 1) * q_rows].astype(jnp.bfloat16)
+                done_ref[0, :, columns] = result[j * q_rows : (j + 1) * q_rows].astype(jnp.bfloat16)
         if mode == "write":
             head = jnp.bitwise_xor(own_head, mask)
             copies.append(
                 pltpu.make_async_copy(
-                    done_ref.at[:, first * DH : (first + count) * DH],
+                    done_ref.at[0, :, first * DH : (first + count) * DH],
                     out_ref.at[:, columns_from(head * GROUP + first, count)],
                     sems.at[1 + first // count],
+                )
+            )
+            copies[-1].start()
+        if mode == "write" and first == 0 and waiting is not None:
+            done_ref[1] = refs[0][0]
+            head = jnp.bitwise_xor(own_head, waiting)
+            copies.append(
+                pltpu.make_async_copy(
+                    done_ref.at[1], out_ref.at[:, columns_from(head * GROUP, GROUP)], sems.at[0]
                 )
             )
             copies[-1].start()
@@ -317,12 +316,9 @@
         out_specs = ANY
         out_shape = jax.ShapeDtypeStruct((q_rows, KVH * wide), jnp.bfloat16)
         scratch = [
-            pltpu.VMEM((q_rows, wide), jnp.bfloat16),
+            pltpu.VMEM((2, q_rows, wide), jnp.bfloat16),
             pltpu.SemaphoreType.DMA((1 + GROUP * q_rows // ROWS,)),
         ]
-    elif mode == "hold":
-        out_specs = VMEM
-        out_shape = pltpu.VMEM((q_rows, wide), jnp.bfloat16)
     else:
         out_specs = [VMEM, VMEM]
         out_shape = [
@@ -406,11 +402,15 @@
     states, rest = lax.optimization_barrier((states, rest))
     rest.update(relayed(rest))
     offset = first.shape[0] * first.shape[1]
-    out = attend(
-        rest, state=states[0], mask=2, mode="write", partial=[out], offset=offset
-    )
+    done, _ = attend(rest, state=states[0], mask=2, mode="state", offset=offset)
     return attend(
-        rest, state=states[1], mask=3, mode="write", partial=[out], offset=offset
+        rest,
+        state=states[1],
+        mask=3,
+        mode="write",
+        partial=[out],
+        offset=offset,
+        waiting=(2, done),
     )
 
 

time: 46.8 us -> 46.8 us (level)
  no operation moved by 1% of the time
where the time goes in v1:
time: 46.8 us; the launch traced here: 46.4 us
  Pallas kernels  16.9 us (36%)
  blocking collectives  13.5 us (29%)
  starting transfers between devices  7.6 us (16%)
  waiting for transfers between devices  6.9 us (15%)
  between operations  0.76 us (2%)
  other arithmetic  0.72 us (2%)
    all_to_all x1, blocking collectives, per_device(): lax.all_to_all(wanted, 'pool', split_axis=0, concat_axis=0, tiled=True)  13.5 us
    pallas_call x6, Pallas kernels, attend_prefix(): pl.pallas_call(functools.partial(prefix_kernel, mask, at, parts, len(piec...  8.52 us
    ppermute x9, waiting for transfers between devices, swap(): return lax.ppermute(array, 'blk', [(i, i ^ mask) for i in range(blks)])  6.9 us
    pallas_call x1, Pallas kernels, attend_span(): pl.pallas_call(functools.partial(span_kernel, masks, parts, rows), grid=(...  5.62 us
    ppermute x9, starting transfers between devices, swap(): return lax.ppermute(array, 'blk', [(i, i ^ mask) for i in range(blks)])  4.1 us
    all_to_all x1, starting transfers between devices, per_device(): lax.all_to_all(picked, 'pool', split_axis=0, concat_axis=0, tiled=True)  3.51 us
    pallas_call x1, Pallas kernels, pick_pages(): pl.pallas_call(pick_kernel, in_specs=[ANY, ANY], out_specs=ANY, out_shape...  2.07 us
  transfers between devices with their start and end apart: 10, of which 4 were waited for; matrix products, arithmetic and copies ran while one was open for 0% of the time, Pallas kernels for 27%

profile of v1, /device:TPU:0, one launch (start us, length us, event | category | flops | bytes accessed | tf_op | source)
XLA Modules:
  0.0 46.4 jit_solution(7667258283668834500)
XLA Ops:
  0.0 0.7 %compare_select_fusion = s32[8,1,8]{2,1,0:T(1,128)S(1)} fusion(s32[8]{0:T(128)} %bitcast.3, s32[8]{0:T(128)} %bitcast.2), kind=kLoop, calls=%fused_computation | loop fusion | flops 128 | bytes 320 | tf_op jit(solution)/shard_map/jit(_where)/select_n | solution.py:361
  0.7 13.5 %all_to_all.10.tables_ref = s32[8,1,8]{2,1,0:T(1,128)S(1)} all-to-all(s32[8,1,8]{2,1,0:T(1,128)S(1)} %compare_select_fusion), channel_id=1, replica_groups=mesh['pool'=8,'blk'=4] {'pool'}, dimensions={0} | all-to-all | bytes 512 | tf_op jit(solution)/shard_map/all_to_all | solution.py:362
  14.3 2.1 %pick_pages.1 = bf16[8,2,64,256]{3,2,1,0:T(8,128)(2,1)} custom-call(s32[8,1,8]{2,1,0:T(1,128)S(1)} %all_to_all.10.tables_ref, bf16[16,64,1024]{2,1,0:T(8,128)(2,1)} %store_ref.1), custom_call_target="tpu_custom_call" | custom-call | tf_op jit(solution)/shard_map/pick_pages/pallas_call | solution.py:83
  16.3 3.5 %all-to-all-start.1 = ((bf16[8,2,64,256]{3,2,1,0:T(8,128)(2,1)}), bf16[8,2,64,256]{3,2,1,0:T(8,128)(2,1)S(1)}, u32[]{:S(2)}, u32[]{:S(2)}) async-start(bf16[8,2,64,256]{3,2,1,0:T(8,128)(2,1)} %pick_pages.1), calls=%async_computation.1 | async-start | bytes 1048576 | tf_op jit(solution)/shard_map/all_to_all | solution.py:365
  19.9 1.6 %collective-permute-start.1 = (bf16[128,1024]{1,0:T(8,128)(2,1)S(1)}, bf16[128,1024]{1,0:T(8,128)(2,1)S(1)}, u32[]{:S(2)}, u32[]{:S(2)}) collective-permute-start(bf16[128,1024]{1,0:T(8,128)(2,1)S(1)} %copy-done), channel_id=1, source_target_pairs={{0,2},{1,3},{2,0},{3,1},{4,6},{5,7},{6,4},{7,5},{8,10},{9,11},{10,... | collective-permute-start | bytes 786440 | tf_op jit(solution)/shard_map/ppermute | solution.py:350
  21.4 5.1 %collective-permute-done.1.refs_2_.refs_6_ = bf16[128,1024]{1,0:T(8,128)(2,1)S(1)} collective-permute-done((bf16[128,1024]{1,0:T(8,128)(2,1)S(1)}, bf16[128,1024]{1,0:T(8,128)(2,1)S(1)}, u32[]{:S(2)}, u32[]{:S(2)}) %collective-permute-start.1) | collective-permute-done | bytes 262176 | tf_op jit(solution)/shard_map/ppermute | solution.py:350
  26.5 0.0 collective-permute-start.2
  27.2 0.0 collective-permute-done.refs_1_.refs_5_
  27.2 0.9 %collective-permute-done.2.refs_3_.refs_7_ = bf16[128,1024]{1,0:T(8,128)(2,1)S(1)} collective-permute-done((bf16[128,1024]{1,0:T(8,128)(2,1)S(1)}, bf16[128,1024]{1,0:T(8,128)(2,1)S(1)}, u32[]{:S(2)}, u32[]{:S(2)}) %collective-permute-start.2) | collective-permute-done | bytes 262176 | tf_op jit(solution)/shard_map/ppermute | solution.py:350
  28.1 5.6 %attend_span.1 = (bf16[4,128,1024]{2,1,0:T(8,128)(2,1)S(1)}, f32[4,128,128]{2,1,0:T(8,128)S(1)}, bf16[4,128,1024]{2,1,0:T(8,128)(2,1)S(1)}, f32[8,512]{1,0:T(8,128)S(1)}) custom-call(s32[1]{0:T(128)S(6)} %copy.11.limit_ref, bf16[128,4096]{1,0:T(8,128)(2,1)} %query_ref.1, bf16[128,1024]{1,0:T(8,128)(2,1)S(1)} %copy-done, ...), custom_call_target="tpu_custom_call" | custom-call | flops 1073741824 | bytes 8388608 | tf_op jit(solution)/shard_map/attend_span/pallas_call | solution.py:197
  33.7 0.7 %order_pages.1 = (bf16[4,64,256]{2,1,0:T(8,128)(2,1)S(1)}, bf16[4,64,256]{2,1,0:T(8,128)(2,1)S(1)}) custom-call(s32[1,8]{1,0:T(1,128)} %owners_ref.1, bf16[8,2,64,256]{3,2,1,0:T(8,128)(2,1)S(1)} %all-to-all-done.1.fetched_ref), custom_call_target="tpu_custom_call" | custom-call | tf_op jit(solution)/shard_map/order_pages/pallas_call | solution.py:119
  34.4 1.6 %collective-permute-start.5 = (bf16[4,64,256]{2,1,0:T(8,128)(2,1)S(1)}, bf16[4,64,256]{2,1,0:T(8,128)(2,1)S(1)}, u32[]{:S(2)}, u32[]{:S(2)}) collective-permute-start(bf16[4,64,256]{2,1,0:T(8,128)(2,1)S(1)} %get-tuple-element.37.refs_0_), channel_id=1, source_target_pairs={{0,2},{1,3},{2,0},{3,1},{4,6},{5,7},{6,4},{7,5},{8,10},{9,11},{10,... | collective-permute-start | bytes 393224 | tf_op jit(solution)/shard_map/ppermute | solution.py:350
  36.0 0.5 %collective-permute-start.7 = (bf16[4,64,256]{2,1,0:T(8,128)(2,1)S(1)}, bf16[4,64,256]{2,1,0:T(8,128)(2,1)S(1)}, u32[]{:S(2)}, u32[]{:S(2)}) collective-permute-start(bf16[4,64,256]{2,1,0:T(8,128)(2,1)S(1)} %get-tuple-element.38.refs_1_), channel_id=1, source_target_pairs={{0,2},{1,3},{2,0},{3,1},{4,6},{5,7},{6,4},{7,5},{8,10},{9,11},{10,... | collective-permute-start | bytes 393224 | tf_op jit(solution)/shard_map/ppermute | solution.py:350
  36.5 0.2 collective-permute-start.4
  36.8 1.8 %attend_prefix.6.refs_6_ = bf16[128,4096]{1,0:T(8,128)(2,1)} custom-call(bf16[4,64,256]{2,1,0:T(8,128)(2,1)S(1)} %get-tuple-element.37.refs_0_, bf16[4,64,256]{2,1,0:T(8,128)(2,1)S(1)} %get-tuple-element.38.refs_1_, bf16[4,128,1024]{2,1,0:T(8,128)(2,1)S(1)} %get-tuple-element.39.refs_2_.refs_1_, bf16[4,128,1024]{2,1,0:T(8,128)(2,1)S(1)} %get-tuple-element.40.refs_3_.refs_2_, ...), custom_call_target="tpu_custom_call" | custom-call | flops 4294967296 | bytes 1048576 | tf_op jit(solution)/shard_map/attend_prefix/pallas_call | solution.py:332
  38.6 0.0 collective-permute-done.3.refs_0_
  38.6 1.8 %attend_prefix.7.refs_6_ = bf16[128,4096]{1,0:T(8,128)(2,1)} custom-call(bf16[4,64,256]{2,1,0:T(8,128)(2,1)S(1)} %collective-permute-done.3.refs_0_, bf16[4,64,256]{2,1,0:T(8,128)(2,1)S(1)} %collective-permute-done.4.refs_1_, bf16[4,128,1024]{2,1,0:T(8,128)(2,1)S(1)} %get-tuple-element.39.refs_2_.refs_1_, ...), custom_call_target="tpu_custom_call", output_to_operand_aliasing={{}: (6, {})} | custom-call | flops 4294967296 | bytes 1048576 | tf_op jit(solution)/shard_map/attend_prefix/pallas_call | solution.py:332
  40.4 0.4 collective-permute-done.5.refs_0_
  40.8 0.9 %attend_prefix.8 = (bf16[1,128,1024]{2,1,0:T(8,128)(2,1)S(1)}, f32[1,128,128]{2,1,0:T(8,128)S(1)}) custom-call(bf16[4,64,256]{2,1,0:T(8,128)(2,1)S(1)} %collective-permute-done.5.refs_0_, bf16[4,128,1024]{2,1,0:T(8,128)(2,1)S(1)} %get-tuple-element.39.refs_2_.refs_1_, bf16[4,128,1024]{2,1,0:T(8,128)(2,1)S(1)} %get-tuple-element.40.refs_3_.refs_2_, ...), custom_call_target="tpu_custom_call" | custom-call | flops 2147483648 | bytes 1048576 | tf_op jit(solution)/shard_map/attend_prefix/pallas_call | solution.py:332
  41.7 0.4 collective-permute-done.6.refs_0_
  42.2 0.9 %attend_prefix.9 = (bf16[1,128,1024]{2,1,0:T(8,128)(2,1)S(1)}, f32[1,128,128]{2,1,0:T(8,128)S(1)}) custom-call(bf16[4,64,256]{2,1,0:T(8,128)(2,1)S(1)} %collective-permute-done.6.refs_0_, bf16[4,128,1024]{2,1,0:T(8,128)(2,1)S(1)} %get-tuple-element.39.refs_2_.refs_1_, bf16[4,128,1024]{2,1,0:T(8,128)(2,1)S(1)} %get-tuple-element.40.refs_3_.refs_2_, ...), custom_call_target="tpu_custom_call" | custom-call | flops 2147483648 | bytes 1048576 | tf_op jit(solution)/shard_map/attend_prefix/pallas_call | solution.py:332
  43.1 0.2 collective-permute-start.8
  43.3 1.5 %attend_prefix.10 = (bf16[1,128,1024]{2,1,0:T(8,128)(2,1)S(1)}, f32[1,128,128]{2,1,0:T(8,128)}) custom-call(bf16[4,64,256]{2,1,0:T(8,128)(2,1)S(1)} %collective-permute-done.7.refs_0_, bf16[4,128,1024]{2,1,0:T(8,128)(2,1)S(1)} %get-tuple-element.39.refs_2_.refs_1_, bf16[1,128,1024]{2,1,0:T(8,128)(2,1)S(1)} %get-tuple-element.51.refs_2_, ...), custom_call_target="tpu_custom_call" | custom-call | flops 2147483648 | bytes 1048576 | tf_op jit(solution)/shard_map/attend_prefix/pallas_call | solution.py:332
  44.8 1.6 %attend_prefix.11 = bf16[128,4096]{1,0:T(8,128)(2,1)} custom-call(bf16[4,64,256]{2,1,0:T(8,128)(2,1)S(1)} %collective-permute-done.8.refs_0_, bf16[4,128,1024]{2,1,0:T(8,128)(2,1)S(1)} %get-tuple-element.39.refs_2_.refs_1_, bf16[1,128,1024]{2,1,0:T(8,128)(2,1)S(1)} %get-tuple-element.49.refs_2_, ...), custom_call_target="tpu_custom_call", output_to_operand_aliasing={{}: (6, {})} | custom-call | flops 2147483648 | bytes 1048576 | tf_op jit(solution)/shard_map/attend_prefix/pallas_call | solution.py:332
  (9 shorter events, 0.0 us)
Async XLA Ops:
  0.0 19.8 %copy-start = (bf16[128,1024]{1,0:T(8,128)(2,1)S(1)}, bf16[128,1024]{1,0:T(8,128)(2,1)}, u32[]{:S(2)}) copy-start(bf16[128,1024]{1,0:T(8,128)(2,1)} %refs_4_) | copy-start | bytes 786436
  16.3 17.4 %all-to-all-start.1 = ((bf16[8,2,64,256]{3,2,1,0:T(8,128)(2,1)}), bf16[8,2,64,256]{3,2,1,0:T(8,128)(2,1)S(1)}, u32[]{:S(2)}, u32[]{:S(2)}) async-start(bf16[8,2,64,256]{3,2,1,0:T(8,128)(2,1)} %pick_pages.1), calls=%async_computation.1 | async-start | bytes 1048576 | tf_op jit(solution)/shard_map/all_to_all | solution.py:365
  19.9 6.7 %collective-permute-start.1 = (bf16[128,1024]{1,0:T(8,128)(2,1)S(1)}, bf16[128,1024]{1,0:T(8,128)(2,1)S(1)}, u32[]{:S(2)}, u32[]{:S(2)}) collective-permute-start(bf16[128,1024]{1,0:T(8,128)(2,1)S(1)} %copy-done), channel_id=1, source_target_pairs={{0,2},{1,3},{2,0},{3,1},{4,6},{5,7},{6,4},{7,5},{8,10},{9,11},{10,... | collective-permute-start | bytes 786440 | tf_op jit(solution)/shard_map/ppermute | solution.py:350
  21.4 5.8 %collective-permute-start = (bf16[128,1024]{1,0:T(8,128)(2,1)S(1)}, bf16[128,1024]{1,0:T(8,128)(2,1)S(1)}, u32[]{:S(2)}, u32[]{:S(2)}) collective-permute-start(bf16[128,1024]{1,0:T(8,128)(2,1)S(1)} %copy-done), channel_id=1, source_target_pairs={{0,1},{1,0},{2,3},{3,2},{4,5},{5,4},{6,7},{7,6},{8,9},{9,8},{10,11... | collective-permute-start | bytes 786440 | tf_op jit(solution)/shard_map/ppermute | solution.py:350
  26.5 1.5 %collective-permute-start.2 = (bf16[128,1024]{1,0:T(8,128)(2,1)S(1)}, bf16[128,1024]{1,0:T(8,128)(2,1)S(1)}, u32[]{:S(2)}, u32[]{:S(2)}) collective-permute-start(bf16[128,1024]{1,0:T(8,128)(2,1)S(1)} %collective-permute-done.1.refs_2_.refs_6_), channel_id=1, source_target_pairs={{0,1},{1,0},{2,3},{3,2},{4,5},{5,4},{6,7},{7,6},{8,9},{9,8},{10,11... | collective-permute-start | bytes 786440 | tf_op jit(solution)/shard_map/ppermute | solution.py:350
  34.4 6.4 %collective-permute-start.5 = (bf16[4,64,256]{2,1,0:T(8,128)(2,1)S(1)}, bf16[4,64,256]{2,1,0:T(8,128)(2,1)S(1)}, u32[]{:S(2)}, u32[]{:S(2)}) collective-permute-start(bf16[4,64,256]{2,1,0:T(8,128)(2,1)S(1)} %get-tuple-element.37.refs_0_), channel_id=1, source_target_pairs={{0,2},{1,3},{2,0},{3,1},{4,6},{5,7},{6,4},{7,5},{8,10},{9,11},{10,... | collective-permute-start | bytes 393224 | tf_op jit(solution)/shard_map/ppermute | solution.py:350
  36.0 2.6 %collective-permute-start.3 = (bf16[4,64,256]{2,1,0:T(8,128)(2,1)S(1)}, bf16[4,64,256]{2,1,0:T(8,128)(2,1)S(1)}, u32[]{:S(2)}, u32[]{:S(2)}) collective-permute-start(bf16[4,64,256]{2,1,0:T(8,128)(2,1)S(1)} %get-tuple-element.37.refs_0_), channel_id=1, source_target_pairs={{0,1},{1,0},{2,3},{3,2},{4,5},{5,4},{6,7},{7,6},{8,9},{9,8},{10,11... | collective-permute-start | bytes 393224 | tf_op jit(solution)/shard_map/ppermute | solution.py:350
  36.0 7.1 %collective-permute-start.7 = (bf16[4,64,256]{2,1,0:T(8,128)(2,1)S(1)}, bf16[4,64,256]{2,1,0:T(8,128)(2,1)S(1)}, u32[]{:S(2)}, u32[]{:S(2)}) collective-permute-start(bf16[4,64,256]{2,1,0:T(8,128)(2,1)S(1)} %get-tuple-element.38.refs_1_), channel_id=1, source_target_pairs={{0,2},{1,3},{2,0},{3,1},{4,6},{5,7},{6,4},{7,5},{8,10},{9,11},{10,... | collective-permute-start | bytes 393224 | tf_op jit(solution)/shard_map/ppermute | solution.py:350
  36.5 2.0 %collective-permute-start.4 = (bf16[4,64,256]{2,1,0:T(8,128)(2,1)S(1)}, bf16[4,64,256]{2,1,0:T(8,128)(2,1)S(1)}, u32[]{:S(2)}, u32[]{:S(2)}) collective-permute-start(bf16[4,64,256]{2,1,0:T(8,128)(2,1)S(1)} %get-tuple-element.38.refs_1_), channel_id=1, source_target_pairs={{0,1},{1,0},{2,3},{3,2},{4,5},{5,4},{6,7},{7,6},{8,9},{9,8},{10,11... | collective-permute-start | bytes 393224 | tf_op jit(solution)/shard_map/ppermute | solution.py:350
  40.8 1.3 %collective-permute-start.6 = (bf16[4,64,256]{2,1,0:T(8,128)(2,1)S(1)}, bf16[4,64,256]{2,1,0:T(8,128)(2,1)S(1)}, u32[]{:S(2)}, u32[]{:S(2)}) collective-permute-start(bf16[4,64,256]{2,1,0:T(8,128)(2,1)S(1)} %collective-permute-done.5.refs_0_), channel_id=1, source_target_pairs={{0,1},{1,0},{2,3},{3,2},{4,5},{5,4},{6,7},{7,6},{8,9},{9,8},{10,11... | collective-permute-start | bytes 393224 | tf_op jit(solution)/shard_map/ppermute | solution.py:350
  43.1 1.8 %collective-permute-start.8 = (bf16[4,64,256]{2,1,0:T(8,128)(2,1)S(1)}, bf16[4,64,256]{2,1,0:T(8,128)(2,1)S(1)}, u32[]{:S(2)}, u32[]{:S(2)}) collective-permute-start(bf16[4,64,256]{2,1,0:T(8,128)(2,1)S(1)} %collective-permute-done.7.refs_0_), channel_id=1, source_target_pairs={{0,1},{1,0},{2,3},{3,2},{4,5},{5,4},{6,7},{7,6},{8,9},{9,8},{10,11... | collective-permute-start | bytes 393224 | tf_op jit(solution)/shard_map/ppermute | solution.py:350

commit v2 on v1

--- a/solution.py
+++ b/solution.py
@@ -238,7 +238,7 @@
     if mode == "write":
         *_, out_ref, done_ref, sems = refs
     else:
-        new_mean_ref, new_level_ref = refs
+        new_mean_ref = refs[0]
     whole = bias_ref.shape[1] // parts
     safe = min(max(whole * 5 // 8 // DH * DH - offset, 0), length)
     lanes = lax.broadcasted_iota(jnp.int32, (q_rows, DH), 1)
@@ -270,80 +270,79 @@
         )
         total = summed[:, DH:] + old
         result = (summed[:, :DH] + mean.astype(jnp.float32) * old) / total
-        if mode == "state":
-            new_level = top + jnp.log2(total)
-            for j, columns in enumerate(heads):
-                part = slice(j * q_rows, (j + 1) * q_rows)
-                new_mean_ref[0, :, columns] = result[part].astype(jnp.bfloat16)
-                levels = jnp.where(lanes == first + j, new_level[part], levels)
-        else:
-            for j, columns in enumerate(heads):
-                done_ref[0, :, columns] = result[j * q_rows : (j + 1) * q_rows].astype(jnp.bfloat16)
+        for j, columns in enumerate(heads):
+            part = slice(j * q_rows, (j + 1) * q_rows)
+            rounded = result[part].astype(jnp.bfloat16)
+            if mode == "write":
+                done_ref[0, :, columns] = rounded
+            else:
+                new_mean_ref[0, :, columns] = rounded
+            if mode == "state":
+                levels = jnp.where(lanes == first + j, (top + jnp.log2(total))[part], levels)
         if mode == "write":
             head = jnp.bitwise_xor(own_head, mask)
             copies.append(
                 pltpu.make_async_copy(
                     done_ref.at[0, :, first * DH : (first + count) * DH],
                     out_ref.at[:, columns_from(head * GROUP + first, count)],
-                    sems.at[1 + first // count],
+                    sems.at[first // count],
                 )
             )
             copies[-1].start()
-        if mode == "write" and first == 0 and waiting is not None:
-            done_ref[1] = refs[0][0]
-            head = jnp.bitwise_xor(own_head, waiting)
-            copies.append(
-                pltpu.make_async_copy(
-                    done_ref.at[1], out_ref.at[:, columns_from(head * GROUP, GROUP)], sems.at[0]
+        if mode == "write" and first == 0:
+            for place, other in enumerate(waiting):
+                done_ref[1 + place] = refs[place][0]
+                head = jnp.bitwise_xor(own_head, other)
+                copies.append(
+                    pltpu.make_async_copy(
+                        done_ref.at[1 + place],
+                        out_ref.at[:, columns_from(head * GROUP, GROUP)],
+                        sems.at[GROUP * q_rows // ROWS + place],
+                    )
                 )
-            )
-            copies[-1].start()
+                copies[-1].start()
     for copy in copies:
         copy.wait()
     if mode == "state":
-        new_level_ref[0] = levels
-
-
-def attend_prefix(held, query, state, bias, mask, mode, partial=(), offset=0, waiting=None):
+        refs[1][0] = levels
+
+
+def attend_prefix(held, query, state, bias, mask, mode, offset=0, waiting=()):
     _, q_rows, wide = query.shape
     groups = [held[at] for at in sorted(held) if at % KVH == mask]
     parts = len(groups)
     pieces = [piece for group in groups for piece in group]
     length = len(pieces) * pieces[0].shape[0] * pieces[0].shape[1]
     at = mask if state[0].shape[0] == KVH else 0
+    mean_shape = pltpu.VMEM((1, q_rows, wide), jnp.bfloat16)
     scratch = []
     if mode == "write":
         out_specs = ANY
         out_shape = jax.ShapeDtypeStruct((q_rows, KVH * wide), jnp.bfloat16)
         scratch = [
-            pltpu.VMEM((2, q_rows, wide), jnp.bfloat16),
-            pltpu.SemaphoreType.DMA((1 + GROUP * q_rows // ROWS,)),
+            pltpu.VMEM((1 + len(waiting), q_rows, wide), jnp.bfloat16),
+            pltpu.SemaphoreType.DMA((GROUP * q_rows // ROWS + len(waiting),)),
         ]
+    elif mode == "mean":
+        out_specs, out_shape = VMEM, mean_shape
     else:
         out_specs = [VMEM, VMEM]
-        out_shape = [
-            pltpu.VMEM((1, q_rows, wide), jnp.bfloat16),
-            pltpu.VMEM((1, q_rows, DH), jnp.float32),
-        ]
-    operands = [*pieces, *[in_vmem(array) for array in (query, *state, bias)]]
-    if waiting is not None:
-        operands.append(in_vmem(waiting[1]))
-    waiting_mask = None if waiting is None else waiting[0]
+        out_shape = [mean_shape, pltpu.VMEM((1, q_rows, DH), jnp.float32)]
+    operands = [query, *state, bias, *[result for _, result in waiting]]
+    operands = [*pieces, *[in_vmem(array) for array in operands]]
+    masks = [other for other, _ in waiting]
     return pl.pallas_call(
-        functools.partial(
-            prefix_kernel, mask, at, parts, len(pieces), offset, mode, waiting_mask
-        ),
-        in_specs=[VMEM] * len(operands) + [ANY] * len(partial),
+        functools.partial(prefix_kernel, mask, at, parts, len(pieces), offset, mode, masks),
+        in_specs=[VMEM] * len(operands),
         out_specs=out_specs,
         out_shape=out_shape,
         scratch_shapes=scratch,
-        input_output_aliases={len(operands): 0} if partial else {},
         cost_estimate=pl.CostEstimate(
             flops=64 * q_rows * wide * length, bytes_accessed=2**20, transcendentals=0
         ),
         compiler_params=pltpu.CompilerParams(vmem_limit_bytes=48 * 2**20),
         name="attend_prefix",
-    )(*operands, *partial)
+    )(*operands)
 
 
 def swap(array, blks, mask):
@@ -392,25 +391,26 @@
     for mask in range(KVH, blks, KVH):
         near[mask] = [swap(first, blks, mask), swap(second, blks, mask)]
     near.update(relayed(near))
-    far, rest = across(first), across(second)
     attend = functools.partial(attend_prefix, query=query, bias=bias)
-    out = attend(near, state=state, mask=0, mode="write")
-    out = attend(near, state=state, mask=1, mode="write", partial=[out])
-    out, far = lax.optimization_barrier((out, far))
+    far = across(first)
+    own = attend(near, state=state, mask=0, mode="mean")
+    second, own = lax.optimization_barrier((second, own))
+    rest = across(second)
+    other = attend(near, state=state, mask=1, mode="mean")
+    own, other, far = lax.optimization_barrier((own, other, far))
     far.update(relayed(far))
     states = [attend(far, state=state, mask=mask, mode="state") for mask in (2, 3)]
     states, rest = lax.optimization_barrier((states, rest))
     rest.update(relayed(rest))
     offset = first.shape[0] * first.shape[1]
-    done, _ = attend(rest, state=states[0], mask=2, mode="state", offset=offset)
+    done = attend(rest, state=states[0], mask=2, mode="mean", offset=offset)
     return attend(
         rest,
         state=states[1],
         mask=3,
         mode="write",
-        partial=[out],
         offset=offset,
-        waiting=(2, done),
+        waiting=((0, own), (1, other), (2, done)),
     )
 
 

time: 46.8 us -> 46.5 us (level)
  Pallas kernels: 16.9 us -> 15 us
  waiting for transfers between devices: 6.9 us -> 8.38 us
    pallas_call x6, Pallas kernels: 8.52 us -> 6.6 us  [attend_prefix(): pl.pallas_call(functools.partial(prefix_kernel, mask, at, parts, len(piec...]
    ppermute x9, waiting for transfers between devices: 6.9 us -> 8.38 us  [swap(): return lax.ppermute(array, 'blk', [(i, i ^ mask) for i in range(blks)])]
  transfers between devices with their start and end apart: 10 -> 10, of which waited for: 4 -> 6; matrix products, arithmetic and copies ran while one was open for 0% -> 0% of each run, Pallas kernels for 27% -> 23%
where the time goes in v2:
time: 46.5 us; the launch traced here: 46.1 us
  Pallas kernels  15 us (32%)
  blocking collectives  13.5 us (29%)
  waiting for transfers between devices  8.38 us (18%)
  starting transfers between devices  7.74 us (17%)
  between operations  0.73 us (2%)
  other arithmetic  0.72 us (2%)
    all_to_all x1, blocking collectives, per_device(): lax.all_to_all(wanted, 'pool', split_axis=0, concat_axis=0, tiled=True)  13.5 us
    ppermute x9, waiting for transfers between devices, swap(): return lax.ppermute(array, 'blk', [(i, i ^ mask) for i in range(blks)])  8.38 us
    pallas_call x6, Pallas kernels, attend_prefix(): pl.pallas_call(functools.partial(prefix_kernel, mask, at, parts, len(piec...  6.6 us
    pallas_call x1, Pallas kernels, attend_span(): pl.pallas_call(functools.partial(span_kernel, masks, parts, rows), grid=(...  5.62 us
    ppermute x9, starting transfers between devices, swap(): return lax.ppermute(array, 'blk', [(i, i ^ mask) for i in range(blks)])  4.23 us
    all_to_all x1, starting transfers between devices, per_device(): lax.all_to_all(picked, 'pool', split_axis=0, concat_axis=0, tiled=True)  3.51 us
    pallas_call x1, Pallas kernels, pick_pages(): pl.pallas_call(pick_kernel, in_specs=[ANY, ANY], out_specs=ANY, out_shape...  2.07 us
  transfers between devices with their start and end apart: 10, of which 6 were waited for; matrix products, arithmetic and copies ran while one was open for 0% of the time, Pallas kernels for 23%

profile of v2, /device:TPU:0, one launch (start us, length us, event | category | flops | bytes accessed | tf_op | source)
XLA Modules:
  0.0 46.1 jit_solution(5055832757669256700)
XLA Ops:
  0.0 0.7 %compare_select_fusion = s32[8,1,8]{2,1,0:T(1,128)S(1)} fusion(s32[8]{0:T(128)} %bitcast.3, s32[8]{0:T(128)} %bitcast.2), kind=kLoop, calls=%fused_computation | loop fusion | flops 128 | bytes 320 | tf_op jit(solution)/shard_map/jit(_where)/select_n | solution.py:360
  0.7 13.5 %all_to_all.10.tables_ref = s32[8,1,8]{2,1,0:T(1,128)S(1)} all-to-all(s32[8,1,8]{2,1,0:T(1,128)S(1)} %compare_select_fusion), channel_id=1, replica_groups=mesh['pool'=8,'blk'=4] {'pool'}, dimensions={0} | all-to-all | bytes 512 | tf_op jit(solution)/shard_map/all_to_all | solution.py:361
  14.3 2.1 %pick_pages.1 = bf16[8,2,64,256]{3,2,1,0:T(8,128)(2,1)} custom-call(s32[8,1,8]{2,1,0:T(1,128)S(1)} %all_to_all.10.tables_ref, bf16[16,64,1024]{2,1,0:T(8,128)(2,1)} %store_ref.1), custom_call_target="tpu_custom_call" | custom-call | tf_op jit(solution)/shard_map/pick_pages/pallas_call | solution.py:83
  16.3 3.5 %all-to-all-start.1 = ((bf16[8,2,64,256]{3,2,1,0:T(8,128)(2,1)}), bf16[8,2,64,256]{3,2,1,0:T(8,128)(2,1)S(1)}, u32[]{:S(2)}, u32[]{:S(2)}) async-start(bf16[8,2,64,256]{3,2,1,0:T(8,128)(2,1)} %pick_pages.1), calls=%async_computation.1 | async-start | bytes 1048576 | tf_op jit(solution)/shard_map/all_to_all | solution.py:364
  19.9 1.6 %collective-permute-start.1 = (bf16[128,1024]{1,0:T(8,128)(2,1)S(1)}, bf16[128,1024]{1,0:T(8,128)(2,1)S(1)}, u32[]{:S(2)}, u32[]{:S(2)}) collective-permute-start(bf16[128,1024]{1,0:T(8,128)(2,1)S(1)} %copy-done), channel_id=1, source_target_pairs={{0,2},{1,3},{2,0},{3,1},{4,6},{5,7},{6,4},{7,5},{8,10},{9,11},{10,... | collective-permute-start | bytes 786440 | tf_op jit(solution)/shard_map/ppermute | solution.py:349
  21.4 5.1 %collective-permute-done.1.refs_2_.refs_6_ = bf16[128,1024]{1,0:T(8,128)(2,1)S(1)} collective-permute-done((bf16[128,1024]{1,0:T(8,128)(2,1)S(1)}, bf16[128,1024]{1,0:T(8,128)(2,1)S(1)}, u32[]{:S(2)}, u32[]{:S(2)}) %collective-permute-start.1) | collective-permute-done | bytes 262176 | tf_op jit(solution)/shard_map/ppermute | solution.py:349
  27.2 0.9 %collective-permute-done.2.refs_3_.refs_7_ = bf16[128,1024]{1,0:T(8,128)(2,1)S(1)} collective-permute-done((bf16[128,1024]{1,0:T(8,128)(2,1)S(1)}, bf16[128,1024]{1,0:T(8,128)(2,1)S(1)}, u32[]{:S(2)}, u32[]{:S(2)}) %collective-permute-start.2) | collective-permute-done | bytes 262176 | tf_op jit(solution)/shard_map/ppermute | solution.py:349
  28.1 5.6 %attend_span.1 = (bf16[4,128,1024]{2,1,0:T(8,128)(2,1)S(1)}, f32[4,128,128]{2,1,0:T(8,128)S(1)}, bf16[4,128,1024]{2,1,0:T(8,128)(2,1)S(1)}, f32[8,512]{1,0:T(8,128)S(1)}) custom-call(s32[1]{0:T(128)S(6)} %copy.7.limit_ref, bf16[128,4096]{1,0:T(8,128)(2,1)} %query_ref.1, bf16[128,1024]{1,0:T(8,128)(2,1)S(1)} %copy-done, ...), custom_call_target="tpu_custom_call" | custom-call | flops 1073741824 | bytes 8388608 | tf_op jit(solution)/shard_map/attend_span/pallas_call | solution.py:197
  33.7 0.0 all-to-all-done.1.fetched_ref
  33.7 0.7 %order_pages.1 = (bf16[4,64,256]{2,1,0:T(8,128)(2,1)S(1)}, bf16[4,64,256]{2,1,0:T(8,128)(2,1)S(1)}) custom-call(s32[1,8]{1,0:T(1,128)} %owners_ref.1, bf16[8,2,64,256]{3,2,1,0:T(8,128)(2,1)S(1)} %all-to-all-done.1.fetched_ref), custom_call_target="tpu_custom_call" | custom-call | tf_op jit(solution)/shard_map/order_pages/pallas_call | solution.py:119
  34.4 1.6 %collective-permute-start.5 = (bf16[4,64,256]{2,1,0:T(8,128)(2,1)S(1)}, bf16[4,64,256]{2,1,0:T(8,128)(2,1)S(1)}, u32[]{:S(2)}, u32[]{:S(2)}) collective-permute-start(bf16[4,64,256]{2,1,0:T(8,128)(2,1)S(1)} %get-tuple-element.40.refs_0_), channel_id=1, source_target_pairs={{0,2},{1,3},{2,0},{3,1},{4,6},{5,7},{6,4},{7,5},{8,10},{9,11},{10,... | collective-permute-start | bytes 393224 | tf_op jit(solution)/shard_map/ppermute | solution.py:349
  36.0 0.0 collective-permute-start.3
  36.0 0.5 %collective-permute-start.4 = (bf16[4,64,256]{2,1,0:T(8,128)(2,1)S(1)}, bf16[4,64,256]{2,1,0:T(8,128)(2,1)S(1)}, u32[]{:S(2)}, u32[]{:S(2)}) collective-permute-start(bf16[4,64,256]{2,1,0:T(8,128)(2,1)S(1)} %get-tuple-element.51.refs_1_), channel_id=1, source_target_pairs={{0,1},{1,0},{2,3},{3,2},{4,5},{5,4},{6,7},{7,6},{8,9},{9,8},{10,11... | collective-permute-start | bytes 393224 | tf_op jit(solution)/shard_map/ppermute | solution.py:349
  36.5 1.1 %attend_prefix.6.refs_5_ = bf16[1,128,1024]{2,1,0:T(8,128)(2,1)S(1)} custom-call(bf16[4,64,256]{2,1,0:T(8,128)(2,1)S(1)} %get-tuple-element.40.refs_0_, bf16[4,64,256]{2,1,0:T(8,128)(2,1)S(1)} %get-tuple-element.51.refs_1_, bf16[4,128,1024]{2,1,0:T(8,128)(2,1)S(1)} %get-tuple-element.41.refs_2_.refs_1_, ...), custom_call_target="tpu_custom_call" | custom-call | flops 4294967296 | bytes 1048576 | tf_op jit(solution)/shard_map/attend_prefix/pallas_call | solution.py:334
  37.6 0.6 %collective-permute-start.7 = (bf16[4,64,256]{2,1,0:T(8,128)(2,1)S(1)}, bf16[4,64,256]{2,1,0:T(8,128)(2,1)S(1)}, u32[]{:S(2)}, u32[]{:S(2)}) collective-permute-start(bf16[4,64,256]{2,1,0:T(8,128)(2,1)S(1)} %get-tuple-element.51.refs_1_), channel_id=1, source_target_pairs={{0,2},{1,3},{2,0},{3,1},{4,6},{5,7},{6,4},{7,5},{8,10},{9,11},{10,... | collective-permute-start | bytes 393224 | tf_op jit(solution)/shard_map/ppermute | solution.py:349
  38.2 1.1 %attend_prefix.7.refs_6_ = bf16[1,128,1024]{2,1,0:T(8,128)(2,1)S(1)} custom-call(bf16[4,64,256]{2,1,0:T(8,128)(2,1)S(1)} %collective-permute-done.3.refs_0_, bf16[4,64,256]{2,1,0:T(8,128)(2,1)S(1)} %collective-permute-done.4.refs_1_, bf16[4,128,1024]{2,1,0:T(8,128)(2,1)S(1)} %get-tuple-element.41.refs_2_.refs_1_, ...), custom_call_target="tpu_custom_call" | custom-call | flops 4294967296 | bytes 1048576 | tf_op jit(solution)/shard_map/attend_prefix/pallas_call | solution.py:334
  39.4 0.7 %collective-permute-done.5.refs_0_ = bf16[4,64,256]{2,1,0:T(8,128)(2,1)S(1)} collective-permute-done((bf16[4,64,256]{2,1,0:T(8,128)(2,1)S(1)}, bf16[4,64,256]{2,1,0:T(8,128)(2,1)S(1)}, u32[]{:S(2)}, u32[]{:S(2)}) %collective-permute-start.5) | collective-permute-done | bytes 131104 | tf_op jit(solution)/shard_map/ppermute | solution.py:349
  40.0 0.9 %attend_prefix.8 = (bf16[1,128,1024]{2,1,0:T(8,128)(2,1)S(1)}, f32[1,128,128]{2,1,0:T(8,128)S(1)}) custom-call(bf16[4,64,256]{2,1,0:T(8,128)(2,1)S(1)} %collective-permute-done.5.refs_0_, bf16[4,128,1024]{2,1,0:T(8,128)(2,1)S(1)} %get-tuple-element.41.refs_2_.refs_1_, bf16[4,128,1024]{2,1,0:T(8,128)(2,1)S(1)} %get-tuple-element.42.refs_3_.refs_2_, ...), custom_call_target="tpu_custom_call" | custom-call | flops 2147483648 | bytes 1048576 | tf_op jit(solution)/shard_map/attend_prefix/pallas_call | solution.py:334
  40.9 0.4 collective-permute-done.6.refs_0_
  41.4 0.9 %attend_prefix.9 = (bf16[1,128,1024]{2,1,0:T(8,128)(2,1)S(1)}, f32[1,128,128]{2,1,0:T(8,128)S(1)}) custom-call(bf16[4,64,256]{2,1,0:T(8,128)(2,1)S(1)} %collective-permute-done.6.refs_0_, bf16[4,128,1024]{2,1,0:T(8,128)(2,1)S(1)} %get-tuple-element.41.refs_2_.refs_1_, bf16[4,128,1024]{2,1,0:T(8,128)(2,1)S(1)} %get-tuple-element.42.refs_3_.refs_2_, ...), custom_call_target="tpu_custom_call" | custom-call | flops 2147483648 | bytes 1048576 | tf_op jit(solution)/shard_map/attend_prefix/pallas_call | solution.py:334
  42.3 0.8 %collective-permute-done.7.refs_0_ = bf16[4,64,256]{2,1,0:T(8,128)(2,1)S(1)} collective-permute-done((bf16[4,64,256]{2,1,0:T(8,128)(2,1)S(1)}, bf16[4,64,256]{2,1,0:T(8,128)(2,1)S(1)}, u32[]{:S(2)}, u32[]{:S(2)}) %collective-permute-start.7) | collective-permute-done | bytes 131104 | tf_op jit(solution)/shard_map/ppermute | solution.py:349
  43.1 0.9 %attend_prefix.10.refs_7_ = bf16[1,128,1024]{2,1,0:T(8,128)(2,1)S(1)} custom-call(bf16[4,64,256]{2,1,0:T(8,128)(2,1)S(1)} %collective-permute-done.7.refs_0_, bf16[4,128,1024]{2,1,0:T(8,128)(2,1)S(1)} %get-tuple-element.41.refs_2_.refs_1_, bf16[1,128,1024]{2,1,0:T(8,128)(2,1)S(1)} %get-tuple-element.57.refs_2_, ...), custom_call_target="tpu_custom_call" | custom-call | flops 2147483648 | bytes 1048576 | tf_op jit(solution)/shard_map/attend_prefix/pallas_call | solution.py:334
  44.0 0.4 collective-permute-done.8.refs_0_
  44.4 1.7 %attend_prefix.11 = bf16[128,4096]{1,0:T(8,128)(2,1)} custom-call(bf16[4,64,256]{2,1,0:T(8,128)(2,1)S(1)} %collective-permute-done.8.refs_0_, bf16[4,128,1024]{2,1,0:T(8,128)(2,1)S(1)} %get-tuple-element.41.refs_2_.refs_1_, bf16[1,128,1024]{2,1,0:T(8,128)(2,1)S(1)} %get-tuple-element.53.refs_2_, f32[1,128,128]{2,1,0:T(8,128)S(1)} %get-tuple-element.54.refs_3_, ...), custom_call_target="tpu_custom_call" | custom-call | flops 2147483648 | bytes 1048576 | tf_op jit(solution)/shard_map/attend_prefix/pallas_call | solution.py:334
  (9 shorter events, 0.0 us)
Async XLA Ops:
  0.0 19.8 %copy-start = (bf16[128,1024]{1,0:T(8,128)(2,1)S(1)}, bf16[128,1024]{1,0:T(8,128)(2,1)}, u32[]{:S(2)}) copy-start(bf16[128,1024]{1,0:T(8,128)(2,1)} %refs_4_) | copy-start | bytes 786436
  16.3 17.4 %all-to-all-start.1 = ((bf16[8,2,64,256]{3,2,1,0:T(8,128)(2,1)}), bf16[8,2,64,256]{3,2,1,0:T(8,128)(2,1)S(1)}, u32[]{:S(2)}, u32[]{:S(2)}) async-start(bf16[8,2,64,256]{3,2,1,0:T(8,128)(2,1)} %pick_pages.1), calls=%async_computation.1 | async-start | bytes 1048576 | tf_op jit(solution)/shard_map/all_to_all | solution.py:364
  19.9 6.7 %collective-permute-start.1 = (bf16[128,1024]{1,0:T(8,128)(2,1)S(1)}, bf16[128,1024]{1,0:T(8,128)(2,1)S(1)}, u32[]{:S(2)}, u32[]{:S(2)}) collective-permute-start(bf16[128,1024]{1,0:T(8,128)(2,1)S(1)} %copy-done), channel_id=1, source_target_pairs={{0,2},{1,3},{2,0},{3,1},{4,6},{5,7},{6,4},{7,5},{8,10},{9,11},{10,... | collective-permute-start | bytes 786440 | tf_op jit(solution)/shard_map/ppermute | solution.py:349
  21.4 5.8 %collective-permute-start = (bf16[128,1024]{1,0:T(8,128)(2,1)S(1)}, bf16[128,1024]{1,0:T(8,128)(2,1)S(1)}, u32[]{:S(2)}, u32[]{:S(2)}) collective-permute-start(bf16[128,1024]{1,0:T(8,128)(2,1)S(1)} %copy-done), channel_id=1, source_target_pairs={{0,1},{1,0},{2,3},{3,2},{4,5},{5,4},{6,7},{7,6},{8,9},{9,8},{10,11... | collective-permute-start | bytes 786440 | tf_op jit(solution)/shard_map/ppermute | solution.py:349
  26.5 1.5 %collective-permute-start.2 = (bf16[128,1024]{1,0:T(8,128)(2,1)S(1)}, bf16[128,1024]{1,0:T(8,128)(2,1)S(1)}, u32[]{:S(2)}, u32[]{:S(2)}) collective-permute-start(bf16[128,1024]{1,0:T(8,128)(2,1)S(1)} %collective-permute-done.1.refs_2_.refs_6_), channel_id=1, source_target_pairs={{0,1},{1,0},{2,3},{3,2},{4,5},{5,4},{6,7},{7,6},{8,9},{9,8},{10,11... | collective-permute-start | bytes 786440 | tf_op jit(solution)/shard_map/ppermute | solution.py:349
  34.4 5.6 %collective-permute-start.5 = (bf16[4,64,256]{2,1,0:T(8,128)(2,1)S(1)}, bf16[4,64,256]{2,1,0:T(8,128)(2,1)S(1)}, u32[]{:S(2)}, u32[]{:S(2)}) collective-permute-start(bf16[4,64,256]{2,1,0:T(8,128)(2,1)S(1)} %get-tuple-element.40.refs_0_), channel_id=1, source_target_pairs={{0,2},{1,3},{2,0},{3,1},{4,6},{5,7},{6,4},{7,5},{8,10},{9,11},{10,... | collective-permute-start | bytes 393224 | tf_op jit(solution)/shard_map/ppermute | solution.py:349
  36.0 2.2 %collective-permute-start.3 = (bf16[4,64,256]{2,1,0:T(8,128)(2,1)S(1)}, bf16[4,64,256]{2,1,0:T(8,128)(2,1)S(1)}, u32[]{:S(2)}, u32[]{:S(2)}) collective-permute-start(bf16[4,64,256]{2,1,0:T(8,128)(2,1)S(1)} %get-tuple-element.40.refs_0_), channel_id=1, source_target_pairs={{0,1},{1,0},{2,3},{3,2},{4,5},{5,4},{6,7},{7,6},{8,9},{9,8},{10,11... | collective-permute-start | bytes 393224 | tf_op jit(solution)/shard_map/ppermute | solution.py:349
  36.0 2.2 %collective-permute-start.4 = (bf16[4,64,256]{2,1,0:T(8,128)(2,1)S(1)}, bf16[4,64,256]{2,1,0:T(8,128)(2,1)S(1)}, u32[]{:S(2)}, u32[]{:S(2)}) collective-permute-start(bf16[4,64,256]{2,1,0:T(8,128)(2,1)S(1)} %get-tuple-element.51.refs_1_), channel_id=1, source_target_pairs={{0,1},{1,0},{2,3},{3,2},{4,5},{5,4},{6,7},{7,6},{8,9},{9,8},{10,11... | collective-permute-start | bytes 393224 | tf_op jit(solution)/shard_map/ppermute | solution.py:349
  37.6 5.5 %collective-permute-start.7 = (bf16[4,64,256]{2,1,0:T(8,128)(2,1)S(1)}, bf16[4,64,256]{2,1,0:T(8,128)(2,1)S(1)}, u32[]{:S(2)}, u32[]{:S(2)}) collective-permute-start(bf16[4,64,256]{2,1,0:T(8,128)(2,1)S(1)} %get-tuple-element.51.refs_1_), channel_id=1, source_target_pairs={{0,2},{1,3},{2,0},{3,1},{4,6},{5,7},{6,4},{7,5},{8,10},{9,11},{10,... | collective-permute-start | bytes 393224 | tf_op jit(solution)/shard_map/ppermute | solution.py:349
  40.0 1.3 %collective-permute-start.6 = (bf16[4,64,256]{2,1,0:T(8,128)(2,1)S(1)}, bf16[4,64,256]{2,1,0:T(8,128)(2,1)S(1)}, u32[]{:S(2)}, u32[]{:S(2)}) collective-permute-start(bf16[4,64,256]{2,1,0:T(8,128)(2,1)S(1)} %collective-permute-done.5.refs_0_), channel_id=1, source_target_pairs={{0,1},{1,0},{2,3},{3,2},{4,5},{5,4},{6,7},{7,6},{8,9},{9,8},{10,11... | collective-permute-start | bytes 393224 | tf_op jit(solution)/shard_map/ppermute | solution.py:349
  43.1 1.3 %collective-permute-start.8 = (bf16[4,64,256]{2,1,0:T(8,128)(2,1)S(1)}, bf16[4,64,256]{2,1,0:T(8,128)(2,1)S(1)}, u32[]{:S(2)}, u32[]{:S(2)}) collective-permute-start(bf16[4,64,256]{2,1,0:T(8,128)(2,1)S(1)} %collective-permute-done.7.refs_0_), channel_id=1, source_target_pairs={{0,1},{1,0},{2,3},{3,2},{4,5},{5,4},{6,7},{7,6},{8,9},{9,8},{10,11... | collective-permute-start | bytes 393224 | tf_op jit(solution)/shard_map/ppermute | solution.py:349

commit v3 on v2

--- a/solution.py
+++ b/solution.py
@@ -27,7 +27,7 @@
     return pl.ds(pl.multiple_of(first * DH, DH), count * DH)
 
 
-def pick_kernel(tables_ref, store_ref, out_ref, table, own, load_sems, sems):
+def pick_kernel(tables_ref, store_ref, out_ref, table, chosen, own, load_sems, sems):
     pools, _, listed = tables_ref.shape
     stored, rows, _ = own.shape
     blk = lax.axis_index("blk")
@@ -46,8 +46,7 @@
             )
     for load in loads:
         load.start()
-    for load in loads:
-        load.wait()
+    loads[0].wait()
 
     def page_copy(request, slot, page):
         return pltpu.make_async_copy(
@@ -65,10 +64,19 @@
         state = (jnp.int32(0), [jnp.int32(0)] * CAP)
         _, pages = lax.fori_loop(0, listed, visit, state, unroll=listed <= 8)
         for slot in range(CAP):
-            page_copy(request, slot, pages[slot]).start()
+            chosen[request, slot] = pages[slot]
         return carry
 
     lax.fori_loop(0, pools, serve, 0)
+    for load in loads[1:]:
+        load.wait()
+
+    def send(request, carry):
+        for slot in range(CAP):
+            page_copy(request, slot, chosen[request, slot]).start()
+        return carry
+
+    lax.fori_loop(0, pools, send, 0)
 
     def finish(request, carry):
         for slot in range(CAP):
@@ -87,6 +95,7 @@
         out_shape=pltpu.HBM((pools, CAP, rows, 2 * DH), kv_store.dtype),
         scratch_shapes=[
             pltpu.SMEM(tables.shape, jnp.int32),
+            pltpu.SMEM((pools, CAP), jnp.int32),
             pltpu.VMEM((kv_store.shape[0], rows, 2 * DH), kv_store.dtype),
             pltpu.SemaphoreType.DMA((1 + 2 * LOADS,)),
             pltpu.SemaphoreType.DMA((pools, CAP)),

time: 46.5 us -> 46.5 us (level)
  no operation moved by 1% of the time
where the time goes in v3:
time: 46.5 us; the launch traced here: 46.1 us
  Pallas kernels  15 us (32%)
  blocking collectives  13.5 us (29%)
  waiting for transfers between devices  8.38 us (18%)
  starting transfers between devices  7.74 us (17%)
  between operations  0.73 us (2%)
  other arithmetic  0.72 us (2%)
    all_to_all x1, blocking collectives, per_device(): lax.all_to_all(wanted, 'pool', split_axis=0, concat_axis=0, tiled=True)  13.5 us
    ppermute x9, waiting for transfers between devices, swap(): return lax.ppermute(array, 'blk', [(i, i ^ mask) for i in range(blks)])  8.38 us
    pallas_call x6, Pallas kernels, attend_prefix(): pl.pallas_call(functools.partial(prefix_kernel, mask, at, parts, len(piec...  6.6 us
    pallas_call x1, Pallas kernels, attend_span(): pl.pallas_call(functools.partial(span_kernel, masks, parts, rows), grid=(...  5.62 us
    ppermute x9, starting transfers between devices, swap(): return lax.ppermute(array, 'blk', [(i, i ^ mask) for i in range(blks)])  4.23 us
    all_to_all x1, starting transfers between devices, per_device(): lax.all_to_all(picked, 'pool', split_axis=0, concat_axis=0, tiled=True)  3.51 us
    pallas_call x1, Pallas kernels, pick_pages(): pl.pallas_call(pick_kernel, in_specs=[ANY, ANY], out_specs=ANY, out_shape...  2.07 us
  transfers between devices with their start and end apart: 10, of which 6 were waited for; matrix products, arithmetic and copies ran while one was open for 0% of the time, Pallas kernels for 23%

profile of v3, /device:TPU:0, one launch (start us, length us, event | category | flops | bytes accessed | tf_op | source)
XLA Modules:
  0.0 46.1 jit_solution(14947859989450611753)
XLA Ops:
  0.0 0.7 %compare_select_fusion = s32[8,1,8]{2,1,0:T(1,128)S(1)} fusion(s32[8]{0:T(128)} %bitcast.3, s32[8]{0:T(128)} %bitcast.2), kind=kLoop, calls=%fused_computation | loop fusion | flops 128 | bytes 320 | tf_op jit(solution)/shard_map/jit(_where)/select_n | solution.py:369
  0.7 13.5 %all_to_all.10.tables_ref = s32[8,1,8]{2,1,0:T(1,128)S(1)} all-to-all(s32[8,1,8]{2,1,0:T(1,128)S(1)} %compare_select_fusion), channel_id=1, replica_groups=mesh['pool'=8,'blk'=4] {'pool'}, dimensions={0} | all-to-all | bytes 512 | tf_op jit(solution)/shard_map/all_to_all | solution.py:370
  14.3 2.1 %pick_pages.1 = bf16[8,2,64,256]{3,2,1,0:T(8,128)(2,1)} custom-call(s32[8,1,8]{2,1,0:T(1,128)S(1)} %all_to_all.10.tables_ref, bf16[16,64,1024]{2,1,0:T(8,128)(2,1)} %store_ref.1), custom_call_target="tpu_custom_call" | custom-call | tf_op jit(solution)/shard_map/pick_pages/pallas_call | solution.py:91
  16.3 3.5 %all-to-all-start.1 = ((bf16[8,2,64,256]{3,2,1,0:T(8,128)(2,1)}), bf16[8,2,64,256]{3,2,1,0:T(8,128)(2,1)S(1)}, u32[]{:S(2)}, u32[]{:S(2)}) async-start(bf16[8,2,64,256]{3,2,1,0:T(8,128)(2,1)} %pick_pages.1), calls=%async_computation.1 | async-start | bytes 1048576 | tf_op jit(solution)/shard_map/all_to_all | solution.py:373
  19.9 1.6 %collective-permute-start.1 = (bf16[128,1024]{1,0:T(8,128)(2,1)S(1)}, bf16[128,1024]{1,0:T(8,128)(2,1)S(1)}, u32[]{:S(2)}, u32[]{:S(2)}) collective-permute-start(bf16[128,1024]{1,0:T(8,128)(2,1)S(1)} %copy-done), channel_id=1, source_target_pairs={{0,2},{1,3},{2,0},{3,1},{4,6},{5,7},{6,4},{7,5},{8,10},{9,11},{10,... | collective-permute-start | bytes 786440 | tf_op jit(solution)/shard_map/ppermute | solution.py:358
  21.4 5.1 %collective-permute-done.1.refs_2_.refs_6_ = bf16[128,1024]{1,0:T(8,128)(2,1)S(1)} collective-permute-done((bf16[128,1024]{1,0:T(8,128)(2,1)S(1)}, bf16[128,1024]{1,0:T(8,128)(2,1)S(1)}, u32[]{:S(2)}, u32[]{:S(2)}) %collective-permute-start.1) | collective-permute-done | bytes 262176 | tf_op jit(solution)/shard_map/ppermute | solution.py:358
  27.2 0.9 %collective-permute-done.2.refs_3_.refs_7_ = bf16[128,1024]{1,0:T(8,128)(2,1)S(1)} collective-permute-done((bf16[128,1024]{1,0:T(8,128)(2,1)S(1)}, bf16[128,1024]{1,0:T(8,128)(2,1)S(1)}, u32[]{:S(2)}, u32[]{:S(2)}) %collective-permute-start.2) | collective-permute-done | bytes 262176 | tf_op jit(solution)/shard_map/ppermute | solution.py:358
  28.1 5.6 %attend_span.1 = (bf16[4,128,1024]{2,1,0:T(8,128)(2,1)S(1)}, f32[4,128,128]{2,1,0:T(8,128)S(1)}, bf16[4,128,1024]{2,1,0:T(8,128)(2,1)S(1)}, f32[8,512]{1,0:T(8,128)S(1)}) custom-call(s32[1]{0:T(128)S(6)} %copy.7.limit_ref, bf16[128,4096]{1,0:T(8,128)(2,1)} %query_ref.1, bf16[128,1024]{1,0:T(8,128)(2,1)S(1)} %copy-done, ...), custom_call_target="tpu_custom_call" | custom-call | flops 1073741824 | bytes 8388608 | tf_op jit(solution)/shard_map/attend_span/pallas_call | solution.py:206
  33.7 0.0 all-to-all-done.1.fetched_ref
  33.7 0.7 %order_pages.1 = (bf16[4,64,256]{2,1,0:T(8,128)(2,1)S(1)}, bf16[4,64,256]{2,1,0:T(8,128)(2,1)S(1)}) custom-call(s32[1,8]{1,0:T(1,128)} %owners_ref.1, bf16[8,2,64,256]{3,2,1,0:T(8,128)(2,1)S(1)} %all-to-all-done.1.fetched_ref), custom_call_target="tpu_custom_call" | custom-call | tf_op jit(solution)/shard_map/order_pages/pallas_call | solution.py:128
  34.4 1.6 %collective-permute-start.5 = (bf16[4,64,256]{2,1,0:T(8,128)(2,1)S(1)}, bf16[4,64,256]{2,1,0:T(8,128)(2,1)S(1)}, u32[]{:S(2)}, u32[]{:S(2)}) collective-permute-start(bf16[4,64,256]{2,1,0:T(8,128)(2,1)S(1)} %get-tuple-element.40.refs_0_), channel_id=1, source_target_pairs={{0,2},{1,3},{2,0},{3,1},{4,6},{5,7},{6,4},{7,5},{8,10},{9,11},{10,... | collective-permute-start | bytes 393224 | tf_op jit(solution)/shard_map/ppermute | solution.py:358
  36.0 0.0 collective-permute-start.3
  36.0 0.5 %collective-permute-start.4 = (bf16[4,64,256]{2,1,0:T(8,128)(2,1)S(1)}, bf16[4,64,256]{2,1,0:T(8,128)(2,1)S(1)}, u32[]{:S(2)}, u32[]{:S(2)}) collective-permute-start(bf16[4,64,256]{2,1,0:T(8,128)(2,1)S(1)} %get-tuple-element.51.refs_1_), channel_id=1, source_target_pairs={{0,1},{1,0},{2,3},{3,2},{4,5},{5,4},{6,7},{7,6},{8,9},{9,8},{10,11... | collective-permute-start | bytes 393224 | tf_op jit(solution)/shard_map/ppermute | solution.py:358
  36.5 1.1 %attend_prefix.6.refs_5_ = bf16[1,128,1024]{2,1,0:T(8,128)(2,1)S(1)} custom-call(bf16[4,64,256]{2,1,0:T(8,128)(2,1)S(1)} %get-tuple-element.40.refs_0_, bf16[4,64,256]{2,1,0:T(8,128)(2,1)S(1)} %get-tuple-element.51.refs_1_, bf16[4,128,1024]{2,1,0:T(8,128)(2,1)S(1)} %get-tuple-element.41.refs_2_.refs_1_, ...), custom_call_target="tpu_custom_call" | custom-call | flops 4294967296 | bytes 1048576 | tf_op jit(solution)/shard_map/attend_prefix/pallas_call | solution.py:343
  37.6 0.6 %collective-permute-start.7 = (bf16[4,64,256]{2,1,0:T(8,128)(2,1)S(1)}, bf16[4,64,256]{2,1,0:T(8,128)(2,1)S(1)}, u32[]{:S(2)}, u32[]{:S(2)}) collective-permute-start(bf16[4,64,256]{2,1,0:T(8,128)(2,1)S(1)} %get-tuple-element.51.refs_1_), channel_id=1, source_target_pairs={{0,2},{1,3},{2,0},{3,1},{4,6},{5,7},{6,4},{7,5},{8,10},{9,11},{10,... | collective-permute-start | bytes 393224 | tf_op jit(solution)/shard_map/ppermute | solution.py:358
  38.2 1.1 %attend_prefix.7.refs_6_ = bf16[1,128,1024]{2,1,0:T(8,128)(2,1)S(1)} custom-call(bf16[4,64,256]{2,1,0:T(8,128)(2,1)S(1)} %collective-permute-done.3.refs_0_, bf16[4,64,256]{2,1,0:T(8,128)(2,1)S(1)} %collective-permute-done.4.refs_1_, bf16[4,128,1024]{2,1,0:T(8,128)(2,1)S(1)} %get-tuple-element.41.refs_2_.refs_1_, ...), custom_call_target="tpu_custom_call" | custom-call | flops 4294967296 | bytes 1048576 | tf_op jit(solution)/shard_map/attend_prefix/pallas_call | solution.py:343
  39.4 0.7 %collective-permute-done.5.refs_0_ = bf16[4,64,256]{2,1,0:T(8,128)(2,1)S(1)} collective-permute-done((bf16[4,64,256]{2,1,0:T(8,128)(2,1)S(1)}, bf16[4,64,256]{2,1,0:T(8,128)(2,1)S(1)}, u32[]{:S(2)}, u32[]{:S(2)}) %collective-permute-start.5) | collective-permute-done | bytes 131104 | tf_op jit(solution)/shard_map/ppermute | solution.py:358
  40.0 0.9 %attend_prefix.8 = (bf16[1,128,1024]{2,1,0:T(8,128)(2,1)S(1)}, f32[1,128,128]{2,1,0:T(8,128)S(1)}) custom-call(bf16[4,64,256]{2,1,0:T(8,128)(2,1)S(1)} %collective-permute-done.5.refs_0_, bf16[4,128,1024]{2,1,0:T(8,128)(2,1)S(1)} %get-tuple-element.41.refs_2_.refs_1_, bf16[4,128,1024]{2,1,0:T(8,128)(2,1)S(1)} %get-tuple-element.42.refs_3_.refs_2_, ...), custom_call_target="tpu_custom_call" | custom-call | flops 2147483648 | bytes 1048576 | tf_op jit(solution)/shard_map/attend_prefix/pallas_call | solution.py:343
  40.9 0.4 collective-permute-done.6.refs_0_
  41.4 0.9 %attend_prefix.9 = (bf16[1,128,1024]{2,1,0:T(8,128)(2,1)S(1)}, f32[1,128,128]{2,1,0:T(8,128)S(1)}) custom-call(bf16[4,64,256]{2,1,0:T(8,128)(2,1)S(1)} %collective-permute-done.6.refs_0_, bf16[4,128,1024]{2,1,0:T(8,128)(2,1)S(1)} %get-tuple-element.41.refs_2_.refs_1_, bf16[4,128,1024]{2,1,0:T(8,128)(2,1)S(1)} %get-tuple-element.42.refs_3_.refs_2_, ...), custom_call_target="tpu_custom_call" | custom-call | flops 2147483648 | bytes 1048576 | tf_op jit(solution)/shard_map/attend_prefix/pallas_call | solution.py:343
  42.3 0.8 %collective-permute-done.7.refs_0_ = bf16[4,64,256]{2,1,0:T(8,128)(2,1)S(1)} collective-permute-done((bf16[4,64,256]{2,1,0:T(8,128)(2,1)S(1)}, bf16[4,64,256]{2,1,0:T(8,128)(2,1)S(1)}, u32[]{:S(2)}, u32[]{:S(2)}) %collective-permute-start.7) | collective-permute-done | bytes 131104 | tf_op jit(solution)/shard_map/ppermute | solution.py:358
  43.1 0.9 %attend_prefix.10.refs_7_ = bf16[1,128,1024]{2,1,0:T(8,128)(2,1)S(1)} custom-call(bf16[4,64,256]{2,1,0:T(8,128)(2,1)S(1)} %collective-permute-done.7.refs_0_, bf16[4,128,1024]{2,1,0:T(8,128)(2,1)S(1)} %get-tuple-element.41.refs_2_.refs_1_, bf16[1,128,1024]{2,1,0:T(8,128)(2,1)S(1)} %get-tuple-element.57.refs_2_, ...), custom_call_target="tpu_custom_call" | custom-call | flops 2147483648 | bytes 1048576 | tf_op jit(solution)/shard_map/attend_prefix/pallas_call | solution.py:343
  44.0 0.4 collective-permute-done.8.refs_0_
  44.4 1.7 %attend_prefix.11 = bf16[128,4096]{1,0:T(8,128)(2,1)} custom-call(bf16[4,64,256]{2,1,0:T(8,128)(2,1)S(1)} %collective-permute-done.8.refs_0_, bf16[4,128,1024]{2,1,0:T(8,128)(2,1)S(1)} %get-tuple-element.41.refs_2_.refs_1_, bf16[1,128,1024]{2,1,0:T(8,128)(2,1)S(1)} %get-tuple-element.53.refs_2_, f32[1,128,128]{2,1,0:T(8,128)S(1)} %get-tuple-element.54.refs_3_, ...), custom_call_target="tpu_custom_call" | custom-call | flops 2147483648 | bytes 1048576 | tf_op jit(solution)/shard_map/attend_prefix/pallas_call | solution.py:343
  (9 shorter events, 0.0 us)
Async XLA Ops:
  0.0 19.8 %copy-start = (bf16[128,1024]{1,0:T(8,128)(2,1)S(1)}, bf16[128,1024]{1,0:T(8,128)(2,1)}, u32[]{:S(2)}) copy-start(bf16[128,1024]{1,0:T(8,128)(2,1)} %refs_4_) | copy-start | bytes 786436
  16.3 17.4 %all-to-all-start.1 = ((bf16[8,2,64,256]{3,2,1,0:T(8,128)(2,1)}), bf16[8,2,64,256]{3,2,1,0:T(8,128)(2,1)S(1)}, u32[]{:S(2)}, u32[]{:S(2)}) async-start(bf16[8,2,64,256]{3,2,1,0:T(8,128)(2,1)} %pick_pages.1), calls=%async_computation.1 | async-start | bytes 1048576 | tf_op jit(solution)/shard_map/all_to_all | solution.py:373
  19.9 6.7 %collective-permute-start.1 = (bf16[128,1024]{1,0:T(8,128)(2,1)S(1)}, bf16[128,1024]{1,0:T(8,128)(2,1)S(1)}, u32[]{:S(2)}, u32[]{:S(2)}) collective-permute-start(bf16[128,1024]{1,0:T(8,128)(2,1)S(1)} %copy-done), channel_id=1, source_target_pairs={{0,2},{1,3},{2,0},{3,1},{4,6},{5,7},{6,4},{7,5},{8,10},{9,11},{10,... | collective-permute-start | bytes 786440 | tf_op jit(solution)/shard_map/ppermute | solution.py:358
  21.4 5.8 %collective-permute-start = (bf16[128,1024]{1,0:T(8,128)(2,1)S(1)}, bf16[128,1024]{1,0:T(8,128)(2,1)S(1)}, u32[]{:S(2)}, u32[]{:S(2)}) collective-permute-start(bf16[128,1024]{1,0:T(8,128)(2,1)S(1)} %copy-done), channel_id=1, source_target_pairs={{0,1},{1,0},{2,3},{3,2},{4,5},{5,4},{6,7},{7,6},{8,9},{9,8},{10,11... | collective-permute-start | bytes 786440 | tf_op jit(solution)/shard_map/ppermute | solution.py:358
  26.5 1.5 %collective-permute-start.2 = (bf16[128,1024]{1,0:T(8,128)(2,1)S(1)}, bf16[128,1024]{1,0:T(8,128)(2,1)S(1)}, u32[]{:S(2)}, u32[]{:S(2)}) collective-permute-start(bf16[128,1024]{1,0:T(8,128)(2,1)S(1)} %collective-permute-done.1.refs_2_.refs_6_), channel_id=1, source_target_pairs={{0,1},{1,0},{2,3},{3,2},{4,5},{5,4},{6,7},{7,6},{8,9},{9,8},{10,11... | collective-permute-start | bytes 786440 | tf_op jit(solution)/shard_map/ppermute | solution.py:358
  34.4 5.6 %collective-permute-start.5 = (bf16[4,64,256]{2,1,0:T(8,128)(2,1)S(1)}, bf16[4,64,256]{2,1,0:T(8,128)(2,1)S(1)}, u32[]{:S(2)}, u32[]{:S(2)}) collective-permute-start(bf16[4,64,256]{2,1,0:T(8,128)(2,1)S(1)} %get-tuple-element.40.refs_0_), channel_id=1, source_target_pairs={{0,2},{1,3},{2,0},{3,1},{4,6},{5,7},{6,4},{7,5},{8,10},{9,11},{10,... | collective-permute-start | bytes 393224 | tf_op jit(solution)/shard_map/ppermute | solution.py:358
  36.0 2.2 %collective-permute-start.3 = (bf16[4,64,256]{2,1,0:T(8,128)(2,1)S(1)}, bf16[4,64,256]{2,1,0:T(8,128)(2,1)S(1)}, u32[]{:S(2)}, u32[]{:S(2)}) collective-permute-start(bf16[4,64,256]{2,1,0:T(8,128)(2,1)S(1)} %get-tuple-element.40.refs_0_), channel_id=1, source_target_pairs={{0,1},{1,0},{2,3},{3,2},{4,5},{5,4},{6,7},{7,6},{8,9},{9,8},{10,11... | collective-permute-start | bytes 393224 | tf_op jit(solution)/shard_map/ppermute | solution.py:358
  36.0 2.2 %collective-permute-start.4 = (bf16[4,64,256]{2,1,0:T(8,128)(2,1)S(1)}, bf16[4,64,256]{2,1,0:T(8,128)(2,1)S(1)}, u32[]{:S(2)}, u32[]{:S(2)}) collective-permute-start(bf16[4,64,256]{2,1,0:T(8,128)(2,1)S(1)} %get-tuple-element.51.refs_1_), channel_id=1, source_target_pairs={{0,1},{1,0},{2,3},{3,2},{4,5},{5,4},{6,7},{7,6},{8,9},{9,8},{10,11... | collective-permute-start | bytes 393224 | tf_op jit(solution)/shard_map/ppermute | solution.py:358
  37.6 5.5 %collective-permute-start.7 = (bf16[4,64,256]{2,1,0:T(8,128)(2,1)S(1)}, bf16[4,64,256]{2,1,0:T(8,128)(2,1)S(1)}, u32[]{:S(2)}, u32[]{:S(2)}) collective-permute-start(bf16[4,64,256]{2,1,0:T(8,128)(2,1)S(1)} %get-tuple-element.51.refs_1_), channel_id=1, source_target_pairs={{0,2},{1,3},{2,0},{3,1},{4,6},{5,7},{6,4},{7,5},{8,10},{9,11},{10,... | collective-permute-start | bytes 393224 | tf_op jit(solution)/shard_map/ppermute | solution.py:358
  40.0 1.3 %collective-permute-start.6 = (bf16[4,64,256]{2,1,0:T(8,128)(2,1)S(1)}, bf16[4,64,256]{2,1,0:T(8,128)(2,1)S(1)}, u32[]{:S(2)}, u32[]{:S(2)}) collective-permute-start(bf16[4,64,256]{2,1,0:T(8,128)(2,1)S(1)} %collective-permute-done.5.refs_0_), channel_id=1, source_target_pairs={{0,1},{1,0},{2,3},{3,2},{4,5},{5,4},{6,7},{7,6},{8,9},{9,8},{10,11... | collective-permute-start | bytes 393224 | tf_op jit(solution)/shard_map/ppermute | solution.py:358
  43.1 1.3 %collective-permute-start.8 = (bf16[4,64,256]{2,1,0:T(8,128)(2,1)S(1)}, bf16[4,64,256]{2,1,0:T(8,128)(2,1)S(1)}, u32[]{:S(2)}, u32[]{:S(2)}) collective-permute-start(bf16[4,64,256]{2,1,0:T(8,128)(2,1)S(1)} %collective-permute-done.7.refs_0_), channel_id=1, source_target_pairs={{0,1},{1,0},{2,3},{3,2},{4,5},{5,4},{6,7},{7,6},{8,9},{9,8},{10,11... | collective-permute-start | bytes 393224 | tf_op jit(solution)/shard_map/ppermute | solution.py:358

commit v4 on v2

--- a/solution.py
+++ b/solution.py
@@ -307,7 +307,7 @@
         refs[1][0] = levels
 
 
-def attend_prefix(held, query, state, bias, mask, mode, offset=0, waiting=()):
+def attend_prefix(held, query, state, bias, mask, mode, offset=0, waiting=(), partial=()):
     _, q_rows, wide = query.shape
     groups = [held[at] for at in sorted(held) if at % KVH == mask]
     parts = len(groups)
@@ -333,16 +333,17 @@
     masks = [other for other, _ in waiting]
     return pl.pallas_call(
         functools.partial(prefix_kernel, mask, at, parts, len(pieces), offset, mode, masks),
-        in_specs=[VMEM] * len(operands),
+        in_specs=[VMEM] * len(operands) + [ANY] * len(partial),
         out_specs=out_specs,
         out_shape=out_shape,
         scratch_shapes=scratch,
+        input_output_aliases={len(operands): 0} if partial else {},
         cost_estimate=pl.CostEstimate(
             flops=64 * q_rows * wide * length, bytes_accessed=2**20, transcendentals=0
         ),
         compiler_params=pltpu.CompilerParams(vmem_limit_bytes=48 * 2**20),
         name="attend_prefix",
-    )(*operands)
+    )(*operands, *partial)
 
 
 def swap(array, blks, mask):
@@ -396,8 +397,8 @@
     own = attend(near, state=state, mask=0, mode="mean")
     second, own = lax.optimization_barrier((second, own))
     rest = across(second)
-    other = attend(near, state=state, mask=1, mode="mean")
-    own, other, far = lax.optimization_barrier((own, other, far))
+    out = attend(near, state=state, mask=1, mode="write", waiting=((0, own),))
+    out, far = lax.optimization_barrier((out, far))
     far.update(relayed(far))
     states = [attend(far, state=state, mask=mask, mode="state") for mask in (2, 3)]
     states, rest = lax.optimization_barrier((states, rest))
@@ -410,7 +411,8 @@
         mask=3,
         mode="write",
         offset=offset,
-        waiting=((0, own), (1, other), (2, done)),
+        waiting=((2, done),),
+        partial=[out],
     )
 
 

time: 46.5 us -> 46.4 us (level)
  waiting for transfers between devices: 8.38 us -> 7.6 us
  Pallas kernels: 15 us -> 15.6 us
    ppermute x9, waiting for transfers between devices: 8.38 us -> 7.6 us  [swap(): return lax.ppermute(array, 'blk', [(i, i ^ mask) for i in range(blks)])]
    pallas_call x6, Pallas kernels: 6.6 us -> 7.23 us  [attend_prefix(): pl.pallas_call(functools.partial(prefix_kernel, mask, at, parts, len(piec...]
  transfers between devices with their start and end apart: 10 -> 10, of which waited for: 6 -> 5; matrix products, arithmetic and copies ran while one was open for 0% -> 0% of each run, Pallas kernels for 23% -> 24%
where the time goes in v4:
time: 46.4 us; the launch traced here: 46 us
  Pallas kernels  15.6 us (34%)
  blocking collectives  13.5 us (29%)
  starting transfers between devices  7.81 us (17%)
  waiting for transfers between devices  7.6 us (16%)
  between operations  0.75 us (2%)
  other arithmetic  0.72 us (2%)
    all_to_all x1, blocking collectives, per_device(): lax.all_to_all(wanted, 'pool', split_axis=0, concat_axis=0, tiled=True)  13.5 us
    ppermute x9, waiting for transfers between devices, swap(): return lax.ppermute(array, 'blk', [(i, i ^ mask) for i in range(blks)])  7.6 us
    pallas_call x6, Pallas kernels, attend_prefix(): pl.pallas_call(functools.partial(prefix_kernel, mask, at, parts, len(piec...  7.23 us
    pallas_call x1, Pallas kernels, attend_span(): pl.pallas_call(functools.partial(span_kernel, masks, parts, rows), grid=(...  5.62 us
    ppermute x9, starting transfers between devices, swap(): return lax.ppermute(array, 'blk', [(i, i ^ mask) for i in range(blks)])  4.3 us
    all_to_all x1, starting transfers between devices, per_device(): lax.all_to_all(picked, 'pool', split_axis=0, concat_axis=0, tiled=True)  3.51 us
    pallas_call x1, Pallas kernels, pick_pages(): pl.pallas_call(pick_kernel, in_specs=[ANY, ANY], out_specs=ANY, out_shape...  2.07 us
  transfers between devices with their start and end apart: 10, of which 5 were waited for; matrix products, arithmetic and copies ran while one was open for 0% of the time, Pallas kernels for 24%

profile of v4, /device:TPU:0, one launch (start us, length us, event | category | flops | bytes accessed | tf_op | source)
XLA Modules:
  0.0 46.0 jit_solution(10193774049922638322)
XLA Ops:
  0.0 0.7 %compare_select_fusion = s32[8,1,8]{2,1,0:T(1,128)S(1)} fusion(s32[8]{0:T(128)} %bitcast.3, s32[8]{0:T(128)} %bitcast.2), kind=kLoop, calls=%fused_computation | loop fusion | flops 128 | bytes 320 | tf_op jit(solution)/shard_map/jit(_where)/select_n | solution.py:361
  0.7 13.5 %all_to_all.10.tables_ref = s32[8,1,8]{2,1,0:T(1,128)S(1)} all-to-all(s32[8,1,8]{2,1,0:T(1,128)S(1)} %compare_select_fusion), channel_id=1, replica_groups=mesh['pool'=8,'blk'=4] {'pool'}, dimensions={0} | all-to-all | bytes 512 | tf_op jit(solution)/shard_map/all_to_all | solution.py:362
  14.3 2.1 %pick_pages.1 = bf16[8,2,64,256]{3,2,1,0:T(8,128)(2,1)} custom-call(s32[8,1,8]{2,1,0:T(1,128)S(1)} %all_to_all.10.tables_ref, bf16[16,64,1024]{2,1,0:T(8,128)(2,1)} %store_ref.1), custom_call_target="tpu_custom_call" | custom-call | tf_op jit(solution)/shard_map/pick_pages/pallas_call | solution.py:83
  16.3 3.5 %all-to-all-start.1 = ((bf16[8,2,64,256]{3,2,1,0:T(8,128)(2,1)}), bf16[8,2,64,256]{3,2,1,0:T(8,128)(2,1)S(1)}, u32[]{:S(2)}, u32[]{:S(2)}) async-start(bf16[8,2,64,256]{3,2,1,0:T(8,128)(2,1)} %pick_pages.1), calls=%async_computation.1 | async-start | bytes 1048576 | tf_op jit(solution)/shard_map/all_to_all | solution.py:365
  19.9 1.6 %collective-permute-start.1 = (bf16[128,1024]{1,0:T(8,128)(2,1)S(1)}, bf16[128,1024]{1,0:T(8,128)(2,1)S(1)}, u32[]{:S(2)}, u32[]{:S(2)}) collective-permute-start(bf16[128,1024]{1,0:T(8,128)(2,1)S(1)} %copy-done), channel_id=1, source_target_pairs={{0,2},{1,3},{2,0},{3,1},{4,6},{5,7},{6,4},{7,5},{8,10},{9,11},{10,... | collective-permute-start | bytes 786440 | tf_op jit(solution)/shard_map/ppermute | solution.py:350
  21.4 5.1 %collective-permute-done.1.refs_2_.refs_6_ = bf16[128,1024]{1,0:T(8,128)(2,1)S(1)} collective-permute-done((bf16[128,1024]{1,0:T(8,128)(2,1)S(1)}, bf16[128,1024]{1,0:T(8,128)(2,1)S(1)}, u32[]{:S(2)}, u32[]{:S(2)}) %collective-permute-start.1) | collective-permute-done | bytes 262176 | tf_op jit(solution)/shard_map/ppermute | solution.py:350
  27.2 0.9 %collective-permute-done.2.refs_3_.refs_7_ = bf16[128,1024]{1,0:T(8,128)(2,1)S(1)} collective-permute-done((bf16[128,1024]{1,0:T(8,128)(2,1)S(1)}, bf16[128,1024]{1,0:T(8,128)(2,1)S(1)}, u32[]{:S(2)}, u32[]{:S(2)}) %collective-permute-start.2) | collective-permute-done | bytes 262176 | tf_op jit(solution)/shard_map/ppermute | solution.py:350
  28.1 5.6 %attend_span.1 = (bf16[4,128,1024]{2,1,0:T(8,128)(2,1)S(1)}, f32[4,128,128]{2,1,0:T(8,128)S(1)}, bf16[4,128,1024]{2,1,0:T(8,128)(2,1)S(1)}, f32[8,512]{1,0:T(8,128)S(1)}) custom-call(s32[1]{0:T(128)S(6)} %copy.9.limit_ref, bf16[128,4096]{1,0:T(8,128)(2,1)} %query_ref.1, bf16[128,1024]{1,0:T(8,128)(2,1)S(1)} %copy-done, ...), custom_call_target="tpu_custom_call" | custom-call | flops 1073741824 | bytes 8388608 | tf_op jit(solution)/shard_map/attend_span/pallas_call | solution.py:197
  33.7 0.0 all-to-all-done.1.fetched_ref
  33.7 0.7 %order_pages.1 = (bf16[4,64,256]{2,1,0:T(8,128)(2,1)S(1)}, bf16[4,64,256]{2,1,0:T(8,128)(2,1)S(1)}) custom-call(s32[1,8]{1,0:T(1,128)} %owners_ref.1, bf16[8,2,64,256]{3,2,1,0:T(8,128)(2,1)S(1)} %all-to-all-done.1.fetched_ref), custom_call_target="tpu_custom_call" | custom-call | tf_op jit(solution)/shard_map/order_pages/pallas_call | solution.py:119
  34.4 1.6 %collective-permute-start.5 = (bf16[4,64,256]{2,1,0:T(8,128)(2,1)S(1)}, bf16[4,64,256]{2,1,0:T(8,128)(2,1)S(1)}, u32[]{:S(2)}, u32[]{:S(2)}) collective-permute-start(bf16[4,64,256]{2,1,0:T(8,128)(2,1)S(1)} %get-tuple-element.38.refs_0_), channel_id=1, source_target_pairs={{0,2},{1,3},{2,0},{3,1},{4,6},{5,7},{6,4},{7,5},{8,10},{9,11},{10,... | collective-permute-start | bytes 393224 | tf_op jit(solution)/shard_map/ppermute | solution.py:350
  36.0 0.0 collective-permute-start.3
  36.0 0.5 %collective-permute-start.4 = (bf16[4,64,256]{2,1,0:T(8,128)(2,1)S(1)}, bf16[4,64,256]{2,1,0:T(8,128)(2,1)S(1)}, u32[]{:S(2)}, u32[]{:S(2)}) collective-permute-start(bf16[4,64,256]{2,1,0:T(8,128)(2,1)S(1)} %get-tuple-element.50.refs_1_), channel_id=1, source_target_pairs={{0,1},{1,0},{2,3},{3,2},{4,5},{5,4},{6,7},{7,6},{8,9},{9,8},{10,11... | collective-permute-start | bytes 393224 | tf_op jit(solution)/shard_map/ppermute | solution.py:350
  36.5 1.1 %attend_prefix.6.refs_6_ = bf16[1,128,1024]{2,1,0:T(8,128)(2,1)S(1)} custom-call(bf16[4,64,256]{2,1,0:T(8,128)(2,1)S(1)} %get-tuple-element.38.refs_0_, bf16[4,64,256]{2,1,0:T(8,128)(2,1)S(1)} %get-tuple-element.50.refs_1_, bf16[4,128,1024]{2,1,0:T(8,128)(2,1)S(1)} %get-tuple-element.40.refs_2_.refs_1_, ...), custom_call_target="tpu_custom_call" | custom-call | flops 4294967296 | bytes 1048576 | tf_op jit(solution)/shard_map/attend_prefix/pallas_call | solution.py:334
  37.6 0.6 %collective-permute-start.7 = (bf16[4,64,256]{2,1,0:T(8,128)(2,1)S(1)}, bf16[4,64,256]{2,1,0:T(8,128)(2,1)S(1)}, u32[]{:S(2)}, u32[]{:S(2)}) collective-permute-start(bf16[4,64,256]{2,1,0:T(8,128)(2,1)S(1)} %get-tuple-element.50.refs_1_), channel_id=1, source_target_pairs={{0,2},{1,3},{2,0},{3,1},{4,6},{5,7},{6,4},{7,5},{8,10},{9,11},{10,... | collective-permute-start | bytes 393224 | tf_op jit(solution)/shard_map/ppermute | solution.py:350
  38.2 1.8 %attend_prefix.7.refs_6_ = bf16[128,4096]{1,0:T(8,128)(2,1)} custom-call(bf16[4,64,256]{2,1,0:T(8,128)(2,1)S(1)} %collective-permute-done.3.refs_0_, bf16[4,64,256]{2,1,0:T(8,128)(2,1)S(1)} %collective-permute-done.4.refs_1_, bf16[4,128,1024]{2,1,0:T(8,128)(2,1)S(1)} %get-tuple-element.40.refs_2_.refs_1_, ...), custom_call_target="tpu_custom_call" | custom-call | flops 4294967296 | bytes 1048576 | tf_op jit(solution)/shard_map/attend_prefix/pallas_call | solution.py:334
  40.1 0.1 collective-permute-start.6
  40.2 0.9 %attend_prefix.8 = (bf16[1,128,1024]{2,1,0:T(8,128)(2,1)S(1)}, f32[1,128,128]{2,1,0:T(8,128)S(1)}) custom-call(bf16[4,64,256]{2,1,0:T(8,128)(2,1)S(1)} %collective-permute-done.5.refs_0_, bf16[4,128,1024]{2,1,0:T(8,128)(2,1)S(1)} %get-tuple-element.40.refs_2_.refs_1_, bf16[4,128,1024]{2,1,0:T(8,128)(2,1)S(1)} %get-tuple-element.41.refs_3_.refs_2_, ...), custom_call_target="tpu_custom_call" | custom-call | flops 2147483648 | bytes 1048576 | tf_op jit(solution)/shard_map/attend_prefix/pallas_call | solution.py:334
  41.1 0.4 collective-permute-done.6.refs_0_
  41.5 0.9 %attend_prefix.9 = (bf16[1,128,1024]{2,1,0:T(8,128)(2,1)S(1)}, f32[1,128,128]{2,1,0:T(8,128)S(1)}) custom-call(bf16[4,64,256]{2,1,0:T(8,128)(2,1)S(1)} %collective-permute-done.6.refs_0_, bf16[4,128,1024]{2,1,0:T(8,128)(2,1)S(1)} %get-tuple-element.40.refs_2_.refs_1_, bf16[4,128,1024]{2,1,0:T(8,128)(2,1)S(1)} %get-tuple-element.41.refs_3_.refs_2_, ...), custom_call_target="tpu_custom_call" | custom-call | flops 2147483648 | bytes 1048576 | tf_op jit(solution)/shard_map/attend_prefix/pallas_call | solution.py:334
  42.4 0.7 %collective-permute-done.7.refs_0_ = bf16[4,64,256]{2,1,0:T(8,128)(2,1)S(1)} collective-permute-done((bf16[4,64,256]{2,1,0:T(8,128)(2,1)S(1)}, bf16[4,64,256]{2,1,0:T(8,128)(2,1)S(1)}, u32[]{:S(2)}, u32[]{:S(2)}) %collective-permute-start.7) | collective-permute-done | bytes 131104 | tf_op jit(solution)/shard_map/ppermute | solution.py:350
  43.1 0.9 %attend_prefix.10.refs_5_ = bf16[1,128,1024]{2,1,0:T(8,128)(2,1)S(1)} custom-call(bf16[4,64,256]{2,1,0:T(8,128)(2,1)S(1)} %collective-permute-done.7.refs_0_, bf16[4,128,1024]{2,1,0:T(8,128)(2,1)S(1)} %get-tuple-element.40.refs_2_.refs_1_, bf16[1,128,1024]{2,1,0:T(8,128)(2,1)S(1)} %get-tuple-element.54.refs_2_, ...), custom_call_target="tpu_custom_call" | custom-call | flops 2147483648 | bytes 1048576 | tf_op jit(solution)/shard_map/attend_prefix/pallas_call | solution.py:334
  44.0 0.4 collective-permute-done.8.refs_0_
  44.4 1.6 %attend_prefix.11 = bf16[128,4096]{1,0:T(8,128)(2,1)} custom-call(bf16[4,64,256]{2,1,0:T(8,128)(2,1)S(1)} %collective-permute-done.8.refs_0_, bf16[4,128,1024]{2,1,0:T(8,128)(2,1)S(1)} %get-tuple-element.40.refs_2_.refs_1_, bf16[1,128,1024]{2,1,0:T(8,128)(2,1)S(1)} %get-tuple-element.52.refs_2_, ...), custom_call_target="tpu_custom_call", output_to_operand_aliasing={{}: (6, {})} | custom-call | flops 2147483648 | bytes 1048576 | tf_op jit(solution)/shard_map/attend_prefix/pallas_call | solution.py:334
  (9 shorter events, 0.0 us)
Async XLA Ops:
  0.0 19.8 %copy-start = (bf16[128,1024]{1,0:T(8,128)(2,1)S(1)}, bf16[128,1024]{1,0:T(8,128)(2,1)}, u32[]{:S(2)}) copy-start(bf16[128,1024]{1,0:T(8,128)(2,1)} %refs_4_) | copy-start | bytes 786436
  16.3 17.4 %all-to-all-start.1 = ((bf16[8,2,64,256]{3,2,1,0:T(8,128)(2,1)}), bf16[8,2,64,256]{3,2,1,0:T(8,128)(2,1)S(1)}, u32[]{:S(2)}, u32[]{:S(2)}) async-start(bf16[8,2,64,256]{3,2,1,0:T(8,128)(2,1)} %pick_pages.1), calls=%async_computation.1 | async-start | bytes 1048576 | tf_op jit(solution)/shard_map/all_to_all | solution.py:365
  19.9 6.7 %collective-permute-start.1 = (bf16[128,1024]{1,0:T(8,128)(2,1)S(1)}, bf16[128,1024]{1,0:T(8,128)(2,1)S(1)}, u32[]{:S(2)}, u32[]{:S(2)}) collective-permute-start(bf16[128,1024]{1,0:T(8,128)(2,1)S(1)} %copy-done), channel_id=1, source_target_pairs={{0,2},{1,3},{2,0},{3,1},{4,6},{5,7},{6,4},{7,5},{8,10},{9,11},{10,... | collective-permute-start | bytes 786440 | tf_op jit(solution)/shard_map/ppermute | solution.py:350
  21.4 5.8 %collective-permute-start = (bf16[128,1024]{1,0:T(8,128)(2,1)S(1)}, bf16[128,1024]{1,0:T(8,128)(2,1)S(1)}, u32[]{:S(2)}, u32[]{:S(2)}) collective-permute-start(bf16[128,1024]{1,0:T(8,128)(2,1)S(1)} %copy-done), channel_id=1, source_target_pairs={{0,1},{1,0},{2,3},{3,2},{4,5},{5,4},{6,7},{7,6},{8,9},{9,8},{10,11... | collective-permute-start | bytes 786440 | tf_op jit(solution)/shard_map/ppermute | solution.py:350
  26.5 1.5 %collective-permute-start.2 = (bf16[128,1024]{1,0:T(8,128)(2,1)S(1)}, bf16[128,1024]{1,0:T(8,128)(2,1)S(1)}, u32[]{:S(2)}, u32[]{:S(2)}) collective-permute-start(bf16[128,1024]{1,0:T(8,128)(2,1)S(1)} %collective-permute-done.1.refs_2_.refs_6_), channel_id=1, source_target_pairs={{0,1},{1,0},{2,3},{3,2},{4,5},{5,4},{6,7},{7,6},{8,9},{9,8},{10,11... | collective-permute-start | bytes 786440 | tf_op jit(solution)/shard_map/ppermute | solution.py:350
  34.4 5.6 %collective-permute-start.5 = (bf16[4,64,256]{2,1,0:T(8,128)(2,1)S(1)}, bf16[4,64,256]{2,1,0:T(8,128)(2,1)S(1)}, u32[]{:S(2)}, u32[]{:S(2)}) collective-permute-start(bf16[4,64,256]{2,1,0:T(8,128)(2,1)S(1)} %get-tuple-element.38.refs_0_), channel_id=1, source_target_pairs={{0,2},{1,3},{2,0},{3,1},{4,6},{5,7},{6,4},{7,5},{8,10},{9,11},{10,... | collective-permute-start | bytes 393224 | tf_op jit(solution)/shard_map/ppermute | solution.py:350
  36.0 2.2 %collective-permute-start.3 = (bf16[4,64,256]{2,1,0:T(8,128)(2,1)S(1)}, bf16[4,64,256]{2,1,0:T(8,128)(2,1)S(1)}, u32[]{:S(2)}, u32[]{:S(2)}) collective-permute-start(bf16[4,64,256]{2,1,0:T(8,128)(2,1)S(1)} %get-tuple-element.38.refs_0_), channel_id=1, source_target_pairs={{0,1},{1,0},{2,3},{3,2},{4,5},{5,4},{6,7},{7,6},{8,9},{9,8},{10,11... | collective-permute-start | bytes 393224 | tf_op jit(solution)/shard_map/ppermute | solution.py:350
  36.0 2.2 %collective-permute-start.4 = (bf16[4,64,256]{2,1,0:T(8,128)(2,1)S(1)}, bf16[4,64,256]{2,1,0:T(8,128)(2,1)S(1)}, u32[]{:S(2)}, u32[]{:S(2)}) collective-permute-start(bf16[4,64,256]{2,1,0:T(8,128)(2,1)S(1)} %get-tuple-element.50.refs_1_), channel_id=1, source_target_pairs={{0,1},{1,0},{2,3},{3,2},{4,5},{5,4},{6,7},{7,6},{8,9},{9,8},{10,11... | collective-permute-start | bytes 393224 | tf_op jit(solution)/shard_map/ppermute | solution.py:350
  37.6 5.5 %collective-permute-start.7 = (bf16[4,64,256]{2,1,0:T(8,128)(2,1)S(1)}, bf16[4,64,256]{2,1,0:T(8,128)(2,1)S(1)}, u32[]{:S(2)}, u32[]{:S(2)}) collective-permute-start(bf16[4,64,256]{2,1,0:T(8,128)(2,1)S(1)} %get-tuple-element.50.refs_1_), channel_id=1, source_target_pairs={{0,2},{1,3},{2,0},{3,1},{4,6},{5,7},{6,4},{7,5},{8,10},{9,11},{10,... | collective-permute-start | bytes 393224 | tf_op jit(solution)/shard_map/ppermute | solution.py:350
  40.1 1.4 %collective-permute-start.6 = (bf16[4,64,256]{2,1,0:T(8,128)(2,1)S(1)}, bf16[4,64,256]{2,1,0:T(8,128)(2,1)S(1)}, u32[]{:S(2)}, u32[]{:S(2)}) collective-permute-start(bf16[4,64,256]{2,1,0:T(8,128)(2,1)S(1)} %collective-permute-done.5.refs_0_), channel_id=1, source_target_pairs={{0,1},{1,0},{2,3},{3,2},{4,5},{5,4},{6,7},{7,6},{8,9},{9,8},{10,11... | collective-permute-start | bytes 393224 | tf_op jit(solution)/shard_map/ppermute | solution.py:350
  43.1 1.3 %collective-permute-start.8 = (bf16[4,64,256]{2,1,0:T(8,128)(2,1)S(1)}, bf16[4,64,256]{2,1,0:T(8,128)(2,1)S(1)}, u32[]{:S(2)}, u32[]{:S(2)}) collective-permute-start(bf16[4,64,256]{2,1,0:T(8,128)(2,1)S(1)} %collective-permute-done.7.refs_0_), channel_id=1, source_target_pairs={{0,1},{1,0},{2,3},{3,2},{4,5},{5,4},{6,7},{7,6},{8,9},{9,8},{10,11... | collective-permute-start | bytes 393224 | tf_op jit(solution)/shard_map/ppermute | solution.py:350

commit v5 on v4

--- a/solution.py
+++ b/solution.py
@@ -15,7 +15,7 @@
 COEF = math.log2(math.e) / math.sqrt(DH)
 LOW = -1e30
 ROWS = 256
-LOADS = 4
+LOADS = 2
 
 
 SMEM = pl.BlockSpec(memory_space=pltpu.SMEM)

time: 46.4 us -> 46.3 us (level)
  no operation moved by 1% of the time
where the time goes in v5:
time: 46.3 us; the launch traced here: 46 us
  Pallas kernels  15.6 us (34%)
  blocking collectives  13.5 us (29%)
  starting transfers between devices  7.81 us (17%)
  waiting for transfers between devices  7.6 us (16%)
  between operations  0.75 us (2%)
  other arithmetic  0.72 us (2%)
    all_to_all x1, blocking collectives, per_device(): lax.all_to_all(wanted, 'pool', split_axis=0, concat_axis=0, tiled=True)  13.5 us
    ppermute x9, waiting for transfers between devices, swap(): return lax.ppermute(array, 'blk', [(i, i ^ mask) for i in range(blks)])  7.6 us
    pallas_call x6, Pallas kernels, attend_prefix(): pl.pallas_call(functools.partial(prefix_kernel, mask, at, parts, len(piec...  7.23 us
    pallas_call x1, Pallas kernels, attend_span(): pl.pallas_call(functools.partial(span_kernel, masks, parts, rows), grid=(...  5.62 us
    ppermute x9, starting transfers between devices, swap(): return lax.ppermute(array, 'blk', [(i, i ^ mask) for i in range(blks)])  4.3 us
    all_to_all x1, starting transfers between devices, per_device(): lax.all_to_all(picked, 'pool', split_axis=0, concat_axis=0, tiled=True)  3.51 us
    pallas_call x1, Pallas kernels, pick_pages(): pl.pallas_call(pick_kernel, in_specs=[ANY, ANY], out_specs=ANY, out_shape...  2.06 us
  transfers between devices with their start and end apart: 10, of which 5 were waited for; matrix products, arithmetic and copies ran while one was open for 0% of the time, Pallas kernels for 24%

profile of v5, /device:TPU:0, one launch (start us, length us, event | category | flops | bytes accessed | tf_op | source)
XLA Modules:
  0.0 46.0 jit_solution(4354768562323104390)
XLA Ops:
  0.0 0.7 %compare_select_fusion = s32[8,1,8]{2,1,0:T(1,128)S(1)} fusion(s32[8]{0:T(128)} %bitcast.3, s32[8]{0:T(128)} %bitcast.2), kind=kLoop, calls=%fused_computation | loop fusion | flops 128 | bytes 320 | tf_op jit(solution)/shard_map/jit(_where)/select_n | solution.py:361
  0.7 13.5 %all_to_all.10.tables_ref = s32[8,1,8]{2,1,0:T(1,128)S(1)} all-to-all(s32[8,1,8]{2,1,0:T(1,128)S(1)} %compare_select_fusion), channel_id=1, replica_groups=mesh['pool'=8,'blk'=4] {'pool'}, dimensions={0} | all-to-all | bytes 512 | tf_op jit(solution)/shard_map/all_to_all | solution.py:362
  14.3 2.1 %pick_pages.1 = bf16[8,2,64,256]{3,2,1,0:T(8,128)(2,1)} custom-call(s32[8,1,8]{2,1,0:T(1,128)S(1)} %all_to_all.10.tables_ref, bf16[16,64,1024]{2,1,0:T(8,128)(2,1)} %store_ref.1), custom_call_target="tpu_custom_call" | custom-call | tf_op jit(solution)/shard_map/pick_pages/pallas_call | solution.py:83
  16.3 3.5 %all-to-all-start.1 = ((bf16[8,2,64,256]{3,2,1,0:T(8,128)(2,1)}), bf16[8,2,64,256]{3,2,1,0:T(8,128)(2,1)S(1)}, u32[]{:S(2)}, u32[]{:S(2)}) async-start(bf16[8,2,64,256]{3,2,1,0:T(8,128)(2,1)} %pick_pages.1), calls=%async_computation.1 | async-start | bytes 1048576 | tf_op jit(solution)/shard_map/all_to_all | solution.py:365
  19.8 1.6 %collective-permute-start.1 = (bf16[128,1024]{1,0:T(8,128)(2,1)S(1)}, bf16[128,1024]{1,0:T(8,128)(2,1)S(1)}, u32[]{:S(2)}, u32[]{:S(2)}) collective-permute-start(bf16[128,1024]{1,0:T(8,128)(2,1)S(1)} %copy-done), channel_id=1, source_target_pairs={{0,2},{1,3},{2,0},{3,1},{4,6},{5,7},{6,4},{7,5},{8,10},{9,11},{10,... | collective-permute-start | bytes 786440 | tf_op jit(solution)/shard_map/ppermute | solution.py:350
  21.4 0.0 collective-permute-start
  21.4 5.1 %collective-permute-done.1.refs_2_.refs_6_ = bf16[128,1024]{1,0:T(8,128)(2,1)S(1)} collective-permute-done((bf16[128,1024]{1,0:T(8,128)(2,1)S(1)}, bf16[128,1024]{1,0:T(8,128)(2,1)S(1)}, u32[]{:S(2)}, u32[]{:S(2)}) %collective-permute-start.1) | collective-permute-done | bytes 262176 | tf_op jit(solution)/shard_map/ppermute | solution.py:350
  26.5 0.0 collective-permute-start.2
  27.2 0.9 %collective-permute-done.2.refs_3_.refs_7_ = bf16[128,1024]{1,0:T(8,128)(2,1)S(1)} collective-permute-done((bf16[128,1024]{1,0:T(8,128)(2,1)S(1)}, bf16[128,1024]{1,0:T(8,128)(2,1)S(1)}, u32[]{:S(2)}, u32[]{:S(2)}) %collective-permute-start.2) | collective-permute-done | bytes 262176 | tf_op jit(solution)/shard_map/ppermute | solution.py:350
  28.1 5.6 %attend_span.1 = (bf16[4,128,1024]{2,1,0:T(8,128)(2,1)S(1)}, f32[4,128,128]{2,1,0:T(8,128)S(1)}, bf16[4,128,1024]{2,1,0:T(8,128)(2,1)S(1)}, f32[8,512]{1,0:T(8,128)S(1)}) custom-call(s32[1]{0:T(128)S(6)} %copy.9.limit_ref, bf16[128,4096]{1,0:T(8,128)(2,1)} %query_ref.1, bf16[128,1024]{1,0:T(8,128)(2,1)S(1)} %copy-done, ...), custom_call_target="tpu_custom_call" | custom-call | flops 1073741824 | bytes 8388608 | tf_op jit(solution)/shard_map/attend_span/pallas_call | solution.py:197
  33.7 0.7 %order_pages.1 = (bf16[4,64,256]{2,1,0:T(8,128)(2,1)S(1)}, bf16[4,64,256]{2,1,0:T(8,128)(2,1)S(1)}) custom-call(s32[1,8]{1,0:T(1,128)} %owners_ref.1, bf16[8,2,64,256]{3,2,1,0:T(8,128)(2,1)S(1)} %all-to-all-done.1.fetched_ref), custom_call_target="tpu_custom_call" | custom-call | tf_op jit(solution)/shard_map/order_pages/pallas_call | solution.py:119
  34.4 1.6 %collective-permute-start.5 = (bf16[4,64,256]{2,1,0:T(8,128)(2,1)S(1)}, bf16[4,64,256]{2,1,0:T(8,128)(2,1)S(1)}, u32[]{:S(2)}, u32[]{:S(2)}) collective-permute-start(bf16[4,64,256]{2,1,0:T(8,128)(2,1)S(1)} %get-tuple-element.38.refs_0_), channel_id=1, source_target_pairs={{0,2},{1,3},{2,0},{3,1},{4,6},{5,7},{6,4},{7,5},{8,10},{9,11},{10,... | collective-permute-start | bytes 393224 | tf_op jit(solution)/shard_map/ppermute | solution.py:350
  36.0 0.5 %collective-permute-start.4 = (bf16[4,64,256]{2,1,0:T(8,128)(2,1)S(1)}, bf16[4,64,256]{2,1,0:T(8,128)(2,1)S(1)}, u32[]{:S(2)}, u32[]{:S(2)}) collective-permute-start(bf16[4,64,256]{2,1,0:T(8,128)(2,1)S(1)} %get-tuple-element.50.refs_1_), channel_id=1, source_target_pairs={{0,1},{1,0},{2,3},{3,2},{4,5},{5,4},{6,7},{7,6},{8,9},{9,8},{10,11... | collective-permute-start | bytes 393224 | tf_op jit(solution)/shard_map/ppermute | solution.py:350
  36.5 1.1 %attend_prefix.6.refs_6_ = bf16[1,128,1024]{2,1,0:T(8,128)(2,1)S(1)} custom-call(bf16[4,64,256]{2,1,0:T(8,128)(2,1)S(1)} %get-tuple-element.38.refs_0_, bf16[4,64,256]{2,1,0:T(8,128)(2,1)S(1)} %get-tuple-element.50.refs_1_, bf16[4,128,1024]{2,1,0:T(8,128)(2,1)S(1)} %get-tuple-element.40.refs_2_.refs_1_, ...), custom_call_target="tpu_custom_call" | custom-call | flops 4294967296 | bytes 1048576 | tf_op jit(solution)/shard_map/attend_prefix/pallas_call | solution.py:334
  37.6 0.6 %collective-permute-start.7 = (bf16[4,64,256]{2,1,0:T(8,128)(2,1)S(1)}, bf16[4,64,256]{2,1,0:T(8,128)(2,1)S(1)}, u32[]{:S(2)}, u32[]{:S(2)}) collective-permute-start(bf16[4,64,256]{2,1,0:T(8,128)(2,1)S(1)} %get-tuple-element.50.refs_1_), channel_id=1, source_target_pairs={{0,2},{1,3},{2,0},{3,1},{4,6},{5,7},{6,4},{7,5},{8,10},{9,11},{10,... | collective-permute-start | bytes 393224 | tf_op jit(solution)/shard_map/ppermute | solution.py:350
  38.2 1.8 %attend_prefix.7.refs_6_ = bf16[128,4096]{1,0:T(8,128)(2,1)} custom-call(bf16[4,64,256]{2,1,0:T(8,128)(2,1)S(1)} %collective-permute-done.3.refs_0_, bf16[4,64,256]{2,1,0:T(8,128)(2,1)S(1)} %collective-permute-done.4.refs_1_, bf16[4,128,1024]{2,1,0:T(8,128)(2,1)S(1)} %get-tuple-element.40.refs_2_.refs_1_, ...), custom_call_target="tpu_custom_call" | custom-call | flops 4294967296 | bytes 1048576 | tf_op jit(solution)/shard_map/attend_prefix/pallas_call | solution.py:334
  40.1 0.1 collective-permute-start.6
  40.2 0.9 %attend_prefix.8 = (bf16[1,128,1024]{2,1,0:T(8,128)(2,1)S(1)}, f32[1,128,128]{2,1,0:T(8,128)S(1)}) custom-call(bf16[4,64,256]{2,1,0:T(8,128)(2,1)S(1)} %collective-permute-done.5.refs_0_, bf16[4,128,1024]{2,1,0:T(8,128)(2,1)S(1)} %get-tuple-element.40.refs_2_.refs_1_, bf16[4,128,1024]{2,1,0:T(8,128)(2,1)S(1)} %get-tuple-element.41.refs_3_.refs_2_, ...), custom_call_target="tpu_custom_call" | custom-call | flops 2147483648 | bytes 1048576 | tf_op jit(solution)/shard_map/attend_prefix/pallas_call | solution.py:334
  41.0 0.4 collective-permute-done.6.refs_0_
  41.5 0.9 %attend_prefix.9 = (bf16[1,128,1024]{2,1,0:T(8,128)(2,1)S(1)}, f32[1,128,128]{2,1,0:T(8,128)S(1)}) custom-call(bf16[4,64,256]{2,1,0:T(8,128)(2,1)S(1)} %collective-permute-done.6.refs_0_, bf16[4,128,1024]{2,1,0:T(8,128)(2,1)S(1)} %get-tuple-element.40.refs_2_.refs_1_, bf16[4,128,1024]{2,1,0:T(8,128)(2,1)S(1)} %get-tuple-element.41.refs_3_.refs_2_, ...), custom_call_target="tpu_custom_call" | custom-call | flops 2147483648 | bytes 1048576 | tf_op jit(solution)/shard_map/attend_prefix/pallas_call | solution.py:334
  42.4 0.7 %collective-permute-done.7.refs_0_ = bf16[4,64,256]{2,1,0:T(8,128)(2,1)S(1)} collective-permute-done((bf16[4,64,256]{2,1,0:T(8,128)(2,1)S(1)}, bf16[4,64,256]{2,1,0:T(8,128)(2,1)S(1)}, u32[]{:S(2)}, u32[]{:S(2)}) %collective-permute-start.7) | collective-permute-done | bytes 131104 | tf_op jit(solution)/shard_map/ppermute | solution.py:350
  43.1 0.9 %attend_prefix.10.refs_5_ = bf16[1,128,1024]{2,1,0:T(8,128)(2,1)S(1)} custom-call(bf16[4,64,256]{2,1,0:T(8,128)(2,1)S(1)} %collective-permute-done.7.refs_0_, bf16[4,128,1024]{2,1,0:T(8,128)(2,1)S(1)} %get-tuple-element.40.refs_2_.refs_1_, bf16[1,128,1024]{2,1,0:T(8,128)(2,1)S(1)} %get-tuple-element.54.refs_2_, ...), custom_call_target="tpu_custom_call" | custom-call | flops 2147483648 | bytes 1048576 | tf_op jit(solution)/shard_map/attend_prefix/pallas_call | solution.py:334
  44.0 0.4 collective-permute-done.8.refs_0_
  44.4 1.6 %attend_prefix.11 = bf16[128,4096]{1,0:T(8,128)(2,1)} custom-call(bf16[4,64,256]{2,1,0:T(8,128)(2,1)S(1)} %collective-permute-done.8.refs_0_, bf16[4,128,1024]{2,1,0:T(8,128)(2,1)S(1)} %get-tuple-element.40.refs_2_.refs_1_, bf16[1,128,1024]{2,1,0:T(8,128)(2,1)S(1)} %get-tuple-element.52.refs_2_, ...), custom_call_target="tpu_custom_call", output_to_operand_aliasing={{}: (6, {})} | custom-call | flops 2147483648 | bytes 1048576 | tf_op jit(solution)/shard_map/attend_prefix/pallas_call | solution.py:334
  (9 shorter events, 0.0 us)
Async XLA Ops:
  0.0 19.8 %copy-start = (bf16[128,1024]{1,0:T(8,128)(2,1)S(1)}, bf16[128,1024]{1,0:T(8,128)(2,1)}, u32[]{:S(2)}) copy-start(bf16[128,1024]{1,0:T(8,128)(2,1)} %refs_4_) | copy-start | bytes 786436
  16.3 17.4 %all-to-all-start.1 = ((bf16[8,2,64,256]{3,2,1,0:T(8,128)(2,1)}), bf16[8,2,64,256]{3,2,1,0:T(8,128)(2,1)S(1)}, u32[]{:S(2)}, u32[]{:S(2)}) async-start(bf16[8,2,64,256]{3,2,1,0:T(8,128)(2,1)} %pick_pages.1), calls=%async_computation.1 | async-start | bytes 1048576 | tf_op jit(solution)/shard_map/all_to_all | solution.py:365
  19.8 6.7 %collective-permute-start.1 = (bf16[128,1024]{1,0:T(8,128)(2,1)S(1)}, bf16[128,1024]{1,0:T(8,128)(2,1)S(1)}, u32[]{:S(2)}, u32[]{:S(2)}) collective-permute-start(bf16[128,1024]{1,0:T(8,128)(2,1)S(1)} %copy-done), channel_id=1, source_target_pairs={{0,2},{1,3},{2,0},{3,1},{4,6},{5,7},{6,4},{7,5},{8,10},{9,11},{10,... | collective-permute-start | bytes 786440 | tf_op jit(solution)/shard_map/ppermute | solution.py:350
  21.4 5.8 %collective-permute-start = (bf16[128,1024]{1,0:T(8,128)(2,1)S(1)}, bf16[128,1024]{1,0:T(8,128)(2,1)S(1)}, u32[]{:S(2)}, u32[]{:S(2)}) collective-permute-start(bf16[128,1024]{1,0:T(8,128)(2,1)S(1)} %copy-done), channel_id=1, source_target_pairs={{0,1},{1,0},{2,3},{3,2},{4,5},{5,4},{6,7},{7,6},{8,9},{9,8},{10,11... | collective-permute-start | bytes 786440 | tf_op jit(solution)/shard_map/ppermute | solution.py:350
  26.5 1.5 %collective-permute-start.2 = (bf16[128,1024]{1,0:T(8,128)(2,1)S(1)}, bf16[128,1024]{1,0:T(8,128)(2,1)S(1)}, u32[]{:S(2)}, u32[]{:S(2)}) collective-permute-start(bf16[128,1024]{1,0:T(8,128)(2,1)S(1)} %collective-permute-done.1.refs_2_.refs_6_), channel_id=1, source_target_pairs={{0,1},{1,0},{2,3},{3,2},{4,5},{5,4},{6,7},{7,6},{8,9},{9,8},{10,11... | collective-permute-start | bytes 786440 | tf_op jit(solution)/shard_map/ppermute | solution.py:350
  34.4 5.6 %collective-permute-start.5 = (bf16[4,64,256]{2,1,0:T(8,128)(2,1)S(1)}, bf16[4,64,256]{2,1,0:T(8,128)(2,1)S(1)}, u32[]{:S(2)}, u32[]{:S(2)}) collective-permute-start(bf16[4,64,256]{2,1,0:T(8,128)(2,1)S(1)} %get-tuple-element.38.refs_0_), channel_id=1, source_target_pairs={{0,2},{1,3},{2,0},{3,1},{4,6},{5,7},{6,4},{7,5},{8,10},{9,11},{10,... | collective-permute-start | bytes 393224 | tf_op jit(solution)/shard_map/ppermute | solution.py:350
  36.0 2.2 %collective-permute-start.3 = (bf16[4,64,256]{2,1,0:T(8,128)(2,1)S(1)}, bf16[4,64,256]{2,1,0:T(8,128)(2,1)S(1)}, u32[]{:S(2)}, u32[]{:S(2)}) collective-permute-start(bf16[4,64,256]{2,1,0:T(8,128)(2,1)S(1)} %get-tuple-element.38.refs_0_), channel_id=1, source_target_pairs={{0,1},{1,0},{2,3},{3,2},{4,5},{5,4},{6,7},{7,6},{8,9},{9,8},{10,11... | collective-permute-start | bytes 393224 | tf_op jit(solution)/shard_map/ppermute | solution.py:350
  36.0 2.2 %collective-permute-start.4 = (bf16[4,64,256]{2,1,0:T(8,128)(2,1)S(1)}, bf16[4,64,256]{2,1,0:T(8,128)(2,1)S(1)}, u32[]{:S(2)}, u32[]{:S(2)}) collective-permute-start(bf16[4,64,256]{2,1,0:T(8,128)(2,1)S(1)} %get-tuple-element.50.refs_1_), channel_id=1, source_target_pairs={{0,1},{1,0},{2,3},{3,2},{4,5},{5,4},{6,7},{7,6},{8,9},{9,8},{10,11... | collective-permute-start | bytes 393224 | tf_op jit(solution)/shard_map/ppermute | solution.py:350
  37.6 5.5 %collective-permute-start.7 = (bf16[4,64,256]{2,1,0:T(8,128)(2,1)S(1)}, bf16[4,64,256]{2,1,0:T(8,128)(2,1)S(1)}, u32[]{:S(2)}, u32[]{:S(2)}) collective-permute-start(bf16[4,64,256]{2,1,0:T(8,128)(2,1)S(1)} %get-tuple-element.50.refs_1_), channel_id=1, source_target_pairs={{0,2},{1,3},{2,0},{3,1},{4,6},{5,7},{6,4},{7,5},{8,10},{9,11},{10,... | collective-permute-start | bytes 393224 | tf_op jit(solution)/shard_map/ppermute | solution.py:350
  40.1 1.4 %collective-permute-start.6 = (bf16[4,64,256]{2,1,0:T(8,128)(2,1)S(1)}, bf16[4,64,256]{2,1,0:T(8,128)(2,1)S(1)}, u32[]{:S(2)}, u32[]{:S(2)}) collective-permute-start(bf16[4,64,256]{2,1,0:T(8,128)(2,1)S(1)} %collective-permute-done.5.refs_0_), channel_id=1, source_target_pairs={{0,1},{1,0},{2,3},{3,2},{4,5},{5,4},{6,7},{7,6},{8,9},{9,8},{10,11... | collective-permute-start | bytes 393224 | tf_op jit(solution)/shard_map/ppermute | solution.py:350
  43.1 1.3 %collective-permute-start.8 = (bf16[4,64,256]{2,1,0:T(8,128)(2,1)S(1)}, bf16[4,64,256]{2,1,0:T(8,128)(2,1)S(1)}, u32[]{:S(2)}, u32[]{:S(2)}) collective-permute-start(bf16[4,64,256]{2,1,0:T(8,128)(2,1)S(1)} %collective-permute-done.7.refs_0_), channel_id=1, source_target_pairs={{0,1},{1,0},{2,3},{3,2},{4,5},{5,4},{6,7},{7,6},{8,9},{9,8},{10,11... | collective-permute-start | bytes 393224 | tf_op jit(solution)/shard_map/ppermute | solution.py:350
